TPU v7x, 512 devices: a whole 4x8x8 slice. The times are simulated.
512 devices in a mesh: ctx: 64 (over y, z), head: 8 (over x, core).
Axes of the slice: x: 4, y: 8, z: 8, core: 2. Of those that a mesh axis runs over, the one named last changes fastest.
Arguments:
- queries: bfloat16 [8192, 2048], P('ctx', 'head'), may hold values from -6 to 6
- key_rows: bfloat16 [8192, 2048], P('ctx', 'head'), may hold values from -6 to 6
- value_rows: bfloat16 [8192, 4096], P('ctx', 'head'), may hold values from -6 to 6
- beta_logit: float32 [8192, 32], P('ctx', 'head'), may hold values from -7 to 2
- log_decay: float32 [8192, 32], P('ctx', 'head'), may hold values from -1 to 0
- out_gate: bfloat16 [8192, 4096], P('ctx', 'head'), may hold values from -6 to 6
- norm_gain: float32 [128], replicated, may hold values from 0.25 to 1.75
- out_weight: bfloat16 [4096, 2048], P('head'), may hold values from -0.09375 to 0.09375
Outputs:
- mixed: bfloat16 [8192, 2048], P('ctx', 'head')
All inputs are finite; a program needn't handle non-finite values.
Results may differ from a plain program's by a relative error of at most 0.005.
Values sent between devices are 32-bit elements; how exact they have to be, the bound alone decides.
A program may use at most 128 MiB of HBM per device.

v0:
```python
import jax
import jax.numpy as jnp
from jax import lax
from jax.sharding import PartitionSpec as P

BLOCK = 64


def carried_in(array, axis, combine, identity):
    size, place = (lax.axis_size(axis), lax.axis_index(axis))
    everything = jax.tree.map(lambda part: lax.all_gather(part, axis), array)
    start = jax.tree.map(
        lambda part, zero: jnp.broadcast_to(jnp.asarray(zero, part.dtype), part.shape),
        array,
        identity,
    )

    def turn(k, before):
        reached = k < place
        new = combine(before, jax.tree.map(lambda part: part[k], everything))
        return jax.tree.map(lambda a, b: jnp.where(reached, a, b), new, before)

    return lax.fori_loop(0, size, turn, start)


def heads_first(values, blocks):
    length_dev, head_count, head_width = values.shape
    return values.reshape(blocks, length_dev // blocks, head_count, head_width).transpose(
        2, 0, 1, 3
    )


def per_device(
    queries, key_rows, value_rows, beta_logit, log_decay, out_gate, norm_gain, out_weight
):
    top_precision = lax.Precision.HIGHEST
    head_width = norm_gain.shape[0]
    length_dev = queries.shape[0]
    head_count = value_rows.shape[1] // head_width
    group_size = head_count // (queries.shape[1] // head_width)
    blocks = length_dev // BLOCK
    query_head = queries.astype(jnp.float32).reshape(length_dev, -1, head_width)
    query_head = heads_first(jnp.repeat(query_head, group_size, axis=1), blocks)
    key_head = key_rows.astype(jnp.float32).reshape(length_dev, -1, head_width)
    key_head = key_head * lax.rsqrt(jnp.sum(key_head * key_head, axis=-1, keepdims=True) + 1e-06)
    key_head = heads_first(jnp.repeat(key_head, group_size, axis=1), blocks)
    value_head = heads_first(
        value_rows.astype(jnp.float32).reshape(length_dev, head_count, head_width), blocks
    )
    beta_head = jax.nn.sigmoid(beta_logit).reshape(blocks, BLOCK, head_count).transpose(2, 0, 1)
    log_cum = jnp.cumsum(log_decay.reshape(blocks, BLOCK, head_count).transpose(2, 0, 1), axis=-1)
    log_total = log_cum[..., -1:]
    position = jnp.arange(BLOCK)
    causal = position[:, None] >= position[None, :]
    strict = position[:, None] > position[None, :]
    log_gap = log_cum[..., :, None] - log_cum[..., None, :]
    decay_mat = jnp.where(causal, jnp.exp(jnp.where(causal, log_gap, 0.0)), 0.0)
    identity_mat = jnp.eye(head_width, dtype=jnp.float32)
    key_gram = jnp.einsum("hnik,hnjk->hnij", key_head, key_head, precision=top_precision)
    system = jnp.eye(BLOCK, dtype=jnp.float32) + jnp.where(
        strict, beta_head[..., :, None] * key_gram * decay_mat, 0.0
    )
    right_value = beta_head[..., None] * value_head
    right_key = (beta_head * jnp.exp(log_cum))[..., None] * key_head
    solved = jax.scipy.linalg.solve_triangular(
        system, jnp.concatenate([right_value, right_key], axis=-1), lower=True
    )
    pseudo = solved[..., :head_width]
    wy_keys = solved[..., head_width:]
    tail_keys = jnp.exp(log_total - log_cum)[..., None] * key_head
    trans_block = jnp.exp(log_total)[..., None] * identity_mat - jnp.einsum(
        "hnck,hncj->hnkj", tail_keys, wy_keys, precision=top_precision
    )
    state_block = jnp.einsum("hnck,hncv->hnkv", tail_keys, pseudo, precision=top_precision)

    def matmul_heads(left_mat, right_mat):
        return jnp.einsum("hij,hjk->hik", left_mat, right_mat, precision=top_precision)

    zero_state = jnp.zeros((head_count, head_width, head_width), jnp.float32)
    start_product = jnp.broadcast_to(identity_mat, (head_count, head_width, head_width))
    trans_seq = jnp.moveaxis(trans_block, 1, 0)
    state_seq = jnp.moveaxis(state_block, 1, 0)
    scores = (
        jnp.einsum("hnik,hnjk->hnij", query_head, key_head, precision=top_precision) * decay_mat
    )
    within = jnp.einsum("hnij,hnjv->hniv", scores, pseudo, precision=top_precision)
    query_map = jnp.exp(log_cum)[..., None] * query_head - jnp.einsum(
        "hnij,hnjk->hnik", scores, wy_keys, precision=top_precision
    )
    within, query_map = (within, query_map)
    map_seq = jnp.moveaxis(query_map, 1, 0)

    def walk_blocks(walk_state, pieces):
        present_state, product = walk_state
        trans_one, sblock, apply_single = pieces
        local_output = jnp.einsum(
            "yfr,yro->yfo", apply_single, present_state, precision=top_precision
        )
        query_eff = jnp.einsum("hck,hkw->hcw", apply_single, product, precision=top_precision)
        present_state = matmul_heads(trans_one, present_state) + sblock
        product = matmul_heads(trans_one, product)
        return ((present_state, product), (local_output, query_eff))

    (local_state, local_trans), (local_seq, effective_sequence) = lax.scan(
        walk_blocks, (zero_state, start_product), (trans_seq, state_seq, map_seq)
    )

    def chain_pairs(earlier, later_pair):
        first_trans, first_state = earlier
        next_trans, next_state = later_pair
        return (
            matmul_heads(next_trans, first_trans),
            matmul_heads(next_trans, first_state) + next_state,
        )

    carried_pair = carried_in(
        (local_trans, local_state), "ctx", chain_pairs, (start_product, zero_state)
    )
    incoming_state = carried_pair[1]
    core_blocks = (
        within
        + jnp.moveaxis(local_seq, 0, 1)
        + jnp.einsum(
            "wgyq,wqb->wgyb",
            jnp.moveaxis(effective_sequence, 0, 1),
            incoming_state,
            precision=top_precision,
        )
    )
    core_out = core_blocks.transpose(1, 2, 0, 3).reshape(length_dev, head_count, head_width)
    gate_head = out_gate.astype(jnp.float32).reshape(length_dev, head_count, head_width)
    normed = core_out * lax.rsqrt(jnp.mean(core_out * core_out, axis=-1, keepdims=True) + 1e-06)
    normed = normed * norm_gain * jax.nn.silu(gate_head)
    gated_out = normed.astype(jnp.bfloat16).reshape(length_dev, head_count * head_width)
    summed = lax.psum_scatter(
        lax.dot_general(
            out_weight, gated_out, (((0,), (1,)), ((), ())), preferred_element_type=jnp.float32
        ),
        "head",
        scatter_dimension=0,
        tiled=True,
    )
    return summed.T.astype(jnp.bfloat16)


def solution(mesh):
    return jax.shard_map(
        per_device,
        mesh=mesh,
        in_specs=(
            P("ctx", "head"),
            P("ctx", "head"),
            P("ctx", "head"),
            P("ctx", "head"),
            P("ctx", "head"),
            P("ctx", "head"),
            P(),
            P("head", None),
        ),
        out_specs=P("ctx", "head"),
        check_vma=False,
    )
```

profile of v0, /device:TPU:57, one launch (start us, length us, event | category | flops | bytes accessed | tf_op | source)
XLA Modules:
  0.0 500.9 jit_solution(1242784959090909143)
XLA Ops:
  11.0 1.7 reshape.95
  15.5 40.0 %custom-call.4 = f32[4,2,1,64,64]{3,4,2,1,0:T(8,128)} custom-call(f32[4,2,1,64,64]{4,3,2,1,0:T(8,128)S(1)} %fusion.40), custom_call_target="InvertDiagBlocksLowerTriangular" | custom-call | tf_op jit(solution)/shard_map/jit(_solve_triangular)/vmap(vmap())/triangular_solve | solution.py:65
  56.6 1.6 fusion.41
  58.2 1.9 convolution_bitcast_fusion.3
  61.3 2.1 fusion.33
  63.3 11.4 %while.31 = (s32[]{:T(128)}, f32[4,128,128]{2,1,0:T(8,128)S(1)}, f32[4,128,128]{2,1,0:T(8,128)S(1)}, f32[2,4,64,128]{3,2,0,1:T(8,128)}, f32[2,4,64,128]{3,2,1,0:...) while((s32[]{:T(128)}, f32[4,128,128]{2,1,0:T(8,128)S(1)}, ...), condition=%wide.region_3.4_spmd.clone, body=%wide.region_2.3_spmd.clone.sunk | while | flops 302186496 | bytes 3936378 | solution.py:104
  63.4 2.0 fusion.102
  66.7 1.9 fusion.103
  69.1 1.9 fusion.102
  72.4 1.9 fusion.103
  76.3 1.5 fusion.34
  77.8 141.8 %all-gather.5.cloned.1.call-done = f32[256,128,128]{2,1,0:T(8,128)} async-done(((f32[4,128,128]{2,1,0:T(8,128)}), f32[256,128,128]{2,1,0:T(8,128)}) %all-gather.5.cloned.1.call-update) | async-done | bytes 16777232 | tf_op jit(solution)/shard_map/all_gather | solution.py:11
  219.6 141.2 %all-gather.7.cloned.1.call-done = f32[256,128,128]{2,1,0:T(8,128)} async-done(((f32[4,128,128]{2,1,0:T(8,128)}), f32[256,128,128]{2,1,0:T(8,128)}) %all-gather.7.cloned.1.call-update) | async-done | bytes 16777232 | tf_op jit(solution)/shard_map/all_gather | solution.py:11
  360.8 94.9 %while.32 = (s32[]{:T(128)}, f32[4,128,128]{2,1,0:T(8,128)S(1)}, s32[]{:T(128)}, f32[64,4,128,128]{3,2,1,0:T(8,128)}, f32[64,4,128,128]{3,2,1,0:T(8,128)}, /*index=5*/s32[]{:T(128)}, s32[]{:T(128)}) while((s32[]{:T(128)}, f32[4,128,128]{2,1,0:T(8,128)S(1)}, s32[]{:T(128)}, f32[64,4,128,128]{3,2,1,0:T(8,128)}, ...), condition=%wide.region_5.6_spmd.clone, body=%wide.region_4.5_spmd.clone.sunk | while | flops 100925440 | bytes 1837671 | solution.py:23
  360.8 1.4 fusion.106
  362.3 1.4 fusion.106
  363.8 1.4 fusion.106
  366.7 1.4 fusion.106
  368.2 1.4 fusion.106
  369.7 1.4 fusion.106
  371.2 1.4 fusion.106
  372.7 1.4 fusion.106
  374.2 1.4 fusion.106
  375.6 1.4 fusion.106
  377.1 1.4 fusion.106
  378.6 1.4 fusion.106
  380.1 1.4 fusion.106
  381.6 1.4 fusion.106
  383.1 1.4 fusion.106
  384.5 1.4 fusion.106
  386.0 1.4 fusion.106
  389.0 1.4 fusion.106
  390.5 1.4 fusion.106
  391.9 1.4 fusion.106
  393.4 1.4 fusion.106
  394.9 1.4 fusion.106
  396.4 1.4 fusion.106
  397.9 1.4 fusion.106
  399.4 1.4 fusion.106
  400.8 1.4 fusion.106
  402.3 1.4 fusion.106
  403.8 1.4 fusion.106
  405.3 1.4 fusion.106
  406.8 1.4 fusion.106
  408.3 1.4 fusion.106
  411.2 1.4 fusion.106
  412.7 1.4 fusion.106
  414.2 1.4 fusion.106
  415.7 1.4 fusion.106
  417.2 1.4 fusion.106
  418.6 1.4 fusion.106
  420.1 1.4 fusion.106
  421.6 1.4 fusion.106
  423.1 1.4 fusion.106
  424.6 1.4 fusion.106
  426.1 1.4 fusion.106
  427.5 1.4 fusion.106
  429.0 1.4 fusion.106
  430.5 1.4 fusion.106
  449.8 1.4 fusion.106
  455.7 1.5 multiply_reduce_fusion
  457.6 2.4 convolution_bitcast_fusion.2
  460.0 32.9 %reduce-scatter.2.cloned.1.call-done = f32[256,128]{0,1:T(8,128)} async-done(((f32[2048,128]{0,1:T(8,128)}), f32[256,128]{0,1:T(8,128)}) %reduce-scatter.2.cloned.1.call-update) | async-done | bytes 131088 | tf_op jit(solution)/shard_map/reduce_scatter | solution.py:135
  492.9 1.5 convert_bitcast_fusion.1
  (141 shorter events, 41.8 us)
Async XLA Ops:
  6.5 451.1 %copy-start = (bf16[512,2048]{1,0:T(8,128)(2,1)S(1)}, bf16[512,2048]{1,0:T(8,128)(2,1)}, u32[]{:S(2)}) copy-start(bf16[512,2048]{1,0:T(8,128)(2,1)} %param.19) | copy-start | bytes 6291460
  6.5 69.7 %copy-start.4 = (f32[128]{0:T(128)S(1)}, f32[128]{0:T(128)}, u32[]{:S(2)}) copy-start(f32[128]{0:T(128)} %param.18) | copy-start | bytes 1540
  6.5 213.1 %all-gather.5.cloned.1.call-start = ((), (), s32[]{:S(2)}) async-start(), calls=%async_computation.2 | async-start | bytes 17039360 | tf_op jit(solution)/shard_map/all_gather | solution.py:11
  58.2 3.0 copy-start.3
  74.7 0.7 copy-start.1
  74.7 0.8 copy-start.2
  75.5 285.3 %all-gather.7.cloned.1.call-start = ((), (), s32[]{:S(2)}) async-start(), calls=%async_computation.3 | async-start | bytes 17039360 | tf_op jit(solution)/shard_map/all_gather | solution.py:11
  76.2 416.7 %reduce-scatter.2.cloned.1.call-start = ((), (), s32[]{:S(2)}) async-start(), calls=%async_computation.1 | async-start | bytes 1179648 | tf_op jit(solution)/shard_map/reduce_scatter | solution.py:135
Sparse Core Ops, SparseCore 0:
  75.6 143.9 all-gather.4
  222.6 138.1 all-gather.6
  460.1 32.6 reduce-scatter.1
where the time goes:
time: 506 us; the launch traced here: 501 us
  waiting for transfers between devices  317 us (63%)
  matrix products  116 us (23%)
  other arithmetic  45.7 us (9%)
  between operations  13.4 us (3%)
  local copies, waits for them, and re-layouts  6.5 us (1%)
    all_gather x2, waiting for transfers between devices, carried_in(): everything = jax.tree.map(lambda part: lax.all_gather(part, axis), array)  283 us
    dot_general x68, matrix products, matmul_heads(): jnp.einsum('hij,hjk->hik', left_mat, right_mat, precision=top_precision)  94.5 us
    another operation x1, other arithmetic, per_device(): jax.scipy.linalg.solve_triangular(system, jnp.concatenate([right_value, r...  40 us
    reduce_scatter x1, waiting for transfers between devices, per_device(): lax.psum_scatter(lax.dot_general(out_weight, gated_out, (((0,), (1,)), ((...  32.9 us
  transfers between devices with their start and end apart: 3, of which 3 were waited for; matrix products, arithmetic and copies ran while one was open for 0% of the time, Pallas kernels for 0%

commit v1 on v0

v1 whole, which is shorter than its diff:
```python
import functools

import jax
import jax.numpy as jnp
from jax import lax
from jax.experimental import pallas as pl
from jax.experimental.pallas import tpu as pltpu
from jax.sharding import PartitionSpec as P

MESH = pl.DeviceIdType.MESH
F32 = jnp.float32
BF16 = jnp.bfloat16
D = 128


def mm(a, b):
    batch = tuple(range(a.ndim - 2))
    dims = (((a.ndim - 1,), (b.ndim - 2,)), (batch, batch))
    return lax.dot_general(a, b, dims, precision=lax.Precision.HIGHEST, preferred_element_type=F32)


def mm_bf16(a, b):
    batch = tuple(range(a.ndim - 2))
    dims = (((a.ndim - 1,), (b.ndim - 2,)), (batch, batch))
    return lax.dot_general(a, b, dims, preferred_element_type=F32)


def mm_split(a, b):
    high = a.astype(BF16)
    low = (a - high.astype(F32)).astype(BF16)
    return mm_bf16(high, b) + mm_bf16(low, b)


def nt(a, b):
    return lax.dot_general(
        a, b, (((1,), (1,)), ((), ())), precision=lax.Precision.HIGHEST, preferred_element_type=F32
    )


def iotas(n):
    return (
        lax.broadcasted_iota(jnp.int32, (n, n), 0),
        lax.broadcasted_iota(jnp.int32, (n, n), 1),
    )


def unit_lower_inverse(strict_part):
    row, col = iotas(D)
    eye = jnp.where(row == col, 1.0, 0.0).astype(F32)

    def off(half):
        shift = half.bit_length() - 1
        rb, cb = row >> shift, col >> shift
        mask = ((rb ^ cb) == 1) & (rb > cb)
        return jnp.where(mask[None], strict_part, 0.0)

    inverse = eye[None] - off(1)
    half = 2
    while half < D:
        inverse = inverse - mm(inverse, mm(off(half), inverse))
        half *= 2
    return inverse


def after(later, earlier):
    both = mm(later[:, :D], earlier)
    return both + jnp.concatenate([jnp.zeros((D, D), F32), later[:, D:]], axis=1)


def ctx_kernel(
    ny,
    nz,
    q_ref,
    k_ref,
    v_ref,
    beta_ref,
    decay_ref,
    gate_ref,
    gain_ref,
    out_ref,
    own,
    zin,
    yin,
    tot_ref,
    prefix,
    sout,
    sin,
    within,
    qmap,
    state_ref,
    zsend,
    zrecv,
    ysend,
    yrecv,
    rsend,
    rrecv,
):
    heads = v_ref.shape[1] // D
    kheads = k_ref.shape[1] // D
    group = heads // kheads
    ctx, head = lax.axis_index("ctx"), lax.axis_index("head")
    y, z, core = ctx // nz, ctx % nz, head % 2
    barrier = pltpu.get_barrier_semaphore()
    for step in range(1, nz):
        pl.semaphore_signal(
            barrier, inc=1, device_id=(y * nz + (z + step) % nz, head), device_id_type=MESH
        )
    for step in range(1, ny):
        pl.semaphore_signal(
            barrier, inc=1, device_id=(((y + step) % ny) * nz + z, head), device_id_type=MESH
        )

    row, col = iotas(D)
    causal, strict = row >= col, row > col
    eye = jnp.where(row == col, 1.0, 0.0).astype(F32)
    tri = jnp.where(causal, 1.0, 0.0).astype(F32)
    keys = jnp.stack([k_ref[:, i * D : (i + 1) * D] for i in range(kheads)])
    queries = jnp.stack([q_ref[:, i * D : (i + 1) * D] for i in range(kheads)])
    values = jnp.stack([v_ref[:, i * D : (i + 1) * D] for i in range(heads)])
    keys32 = keys.astype(F32)
    keys_t32 = jnp.stack([keys32[i].T for i in range(kheads)])
    keys_t = keys_t32.astype(BF16)
    r_col = lax.rsqrt(jnp.sum(keys32 * keys32, axis=2, keepdims=True) + 1e-06)
    r_row = lax.rsqrt(jnp.sum(keys_t32 * keys_t32, axis=1, keepdims=True) + 1e-06)
    gram = mm_bf16(keys, keys_t) * (r_col * r_row)
    scores = mm_bf16(queries, keys_t) * r_row

    beta_row = jax.nn.sigmoid(beta_ref[...])
    decay_row = decay_ref[...]
    cum_row = nt(decay_row, tri)
    cum_col = nt(tri, decay_row)
    beta_col = nt(eye, beta_row)
    exp_row = jnp.exp(cum_row)
    exp_col = jnp.exp(cum_col)
    total = cum_row[:, D - 1 : D]
    exp_total = jnp.exp(total)
    tail_row = jnp.exp(total - cum_row)

    def per_head(fn):
        return jnp.stack([fn(h) for h in range(heads)])

    decay_mat = per_head(
        lambda h: jnp.exp(
            jnp.where(causal, cum_col[:, h : h + 1] - cum_row[h : h + 1, :], -1e30)
        )
    )
    strict_part = per_head(
        lambda h: jnp.where(
            strict, beta_col[:, h : h + 1] * gram[h // group] * decay_mat[h], 0.0
        )
    )
    inverse = unit_lower_inverse(strict_part)
    scaled = per_head(lambda h: inverse[h] * beta_row[h : h + 1, :])
    pseudo = mm_split(scaled, values)
    wy = mm_split(
        per_head(lambda h: scaled[h] * (exp_row[h : h + 1, :] * r_row[h // group])),
        per_head(lambda h: keys[h // group]),
    )
    wy_pseudo = jnp.concatenate([wy, pseudo], axis=2)
    tails = per_head(
        lambda h: keys_t32[h // group] * (r_row[h // group] * tail_row[h : h + 1, :])
    )
    block = mm(tails, wy_pseudo)
    for h in range(heads):
        own[h, :, :D] = exp_total[h : h + 1, :] * eye - block[h, :, :D]
        own[h, :, D:] = block[h, :, D:]

    pl.semaphore_wait(barrier, nz - 1 + ny - 1)

    def head_copy(h):
        return pltpu.make_async_remote_copy(
            src_ref=own.at[h],
            dst_ref=zin.at[z],
            send_sem=zsend.at[h],
            recv_sem=zrecv.at[z],
            device_id=(y * nz + 2 * h + core, head),
            device_id_type=MESH,
        )

    for h in range(heads):
        @pl.when(z != 2 * h + core)
        def _():
            head_copy(h).start()

        @pl.when(z == 2 * h + core)
        def _():
            zin[pl.ds(z, 1)] = own[h : h + 1]

    mixed = mm(per_head(lambda h: scores[h // group] * decay_mat[h]), wy_pseudo)
    for h in range(heads):
        within[h] = mixed[h, :, D:]
        qmap[h] = exp_col[:, h : h + 1] * queries[h // group].astype(F32) - mixed[h, :, :D]

    worker = (z % 2) == core

    def total_copy(target):
        return pltpu.make_async_remote_copy(
            src_ref=tot_ref,
            dst_ref=yin.at[y],
            send_sem=ysend.at[target],
            recv_sem=yrecv.at[y],
            device_id=(target * nz + z, head),
            device_id_type=MESH,
        )

    def state_copy(target):
        return pltpu.make_async_remote_copy(
            src_ref=sout.at[target],
            dst_ref=sin.at[z // 2],
            send_sem=rsend.at[target],
            recv_sem=rrecv.at[z // 2],
            device_id=(y * nz + target, head),
            device_id_type=MESH,
        )

    @pl.when(worker)
    def _():
        for i in range(nz):
            @pl.when(z != i)
            def _():
                pltpu.make_async_remote_copy(
                    src_ref=own.at[0],
                    dst_ref=zin.at[i],
                    send_sem=zsend.at[0],
                    recv_sem=zrecv.at[i],
                    device_id=(ctx, head),
                    device_id_type=MESH,
                ).wait_recv()

        level = {(i, i + 1): zin[i] for i in range(nz)}
        span = 1
        while span < nz:
            for i in range(0, nz, 2 * span):
                level[(i, i + 2 * span)] = after(
                    level[(i + span, i + 2 * span)], level[(i, i + span)]
                )
            span *= 2
        tot_ref[...] = level[(0, nz)]
        for target in range(1, ny):
            @pl.when(target > y)
            def _():
                total_copy(target).start()

        for i in range(1, nz):
            if (0, i) not in level:
                low = 1 << (i.bit_length() - 1)
                rest = i - low
                part = (low, i)
                if part not in level:
                    step = rest & -rest
                    level[part] = None
                    level[(0, i)] = after(level[(i - step, i)], level[(0, i - step)])
                else:
                    level[(0, i)] = after(level[part], level[(0, low)])
            prefix[i] = level[(0, i)]

        state_ref[...] = jnp.zeros((D, D), F32)
        for i in range(ny - 1):
            @pl.when(i < y)
            def _():
                pltpu.make_async_remote_copy(
                    src_ref=tot_ref,
                    dst_ref=yin.at[i],
                    send_sem=ysend.at[0],
                    recv_sem=yrecv.at[i],
                    device_id=(ctx, head),
                    device_id_type=MESH,
                ).wait_recv()
                state_ref[...] = mm(yin[i, :, :D], state_ref[...]) + yin[i, :, D:]

        state = state_ref[...]
        for i in range(nz):
            if i == 0:
                sout[i] = state
            else:
                sout[i] = mm(prefix[i, :, :D], state) + prefix[i, :, D:]

            @pl.when(z != i)
            def _():
                state_copy(i).start()

            @pl.when(z == i)
            def _():
                sin[pl.ds(z // 2, 1)] = sout[i : i + 1]

    for h in range(heads):
        @pl.when(z != 2 * h + core)
        def _():
            pltpu.make_async_remote_copy(
                src_ref=sout.at[0],
                dst_ref=sin.at[h],
                send_sem=rsend.at[0],
                recv_sem=rrecv.at[h],
                device_id=(ctx, head),
                device_id_type=MESH,
            ).wait_recv()

    core_out = within[...] + mm(qmap[...], sin[...])
    normed = core_out * lax.rsqrt(jnp.mean(core_out * core_out, axis=2, keepdims=True) + 1e-06)
    for h in range(heads):
        gate = gate_ref[:, h * D : (h + 1) * D].astype(F32)
        out_ref[:, h * D : (h + 1) * D] = (
            normed[h] * gain_ref[...] * (gate / (1.0 + jnp.exp(-gate)))
        ).astype(BF16)

    for h in range(heads):
        @pl.when(z != 2 * h + core)
        def _():
            head_copy(h).wait_send()

    @pl.when(worker)
    def _():
        for target in range(1, ny):
            @pl.when(target > y)
            def _():
                total_copy(target).wait_send()
        for i in range(nz):
            @pl.when(z != i)
            def _():
                state_copy(i).wait_send()


def head_kernel(
    n, gated_ref, weight_ref, out_ref, pair_out, pair_in, mine, chip_in, psend, precv, csend, crecv
):
    chips = n // 2
    width = out_ref.shape[1]
    ctx, head = lax.axis_index("ctx"), lax.axis_index("head")
    x, core = head // 2, head % 2
    sibling = x * 2 + 1 - core
    barrier = pltpu.get_barrier_semaphore()
    pl.semaphore_signal(barrier, inc=1, device_id=(ctx, sibling), device_id_type=MESH)
    for step in range(1, chips):
        pl.semaphore_signal(
            barrier,
            inc=1,
            device_id=(ctx, ((x + step) % chips) * 2 + core),
            device_id_type=MESH,
        )
    gated = gated_ref[...]

    def columns(chip, which):
        start = pl.multiple_of((chip * 2 + which) * width, width)
        return mm_bf16(gated, weight_ref[:, pl.ds(start, width)])

    def pair_copy(step):
        return pltpu.make_async_remote_copy(
            src_ref=pair_out.at[step],
            dst_ref=pair_in.at[step],
            send_sem=psend.at[step],
            recv_sem=precv.at[step],
            device_id=(ctx, sibling),
            device_id_type=MESH,
        )

    def chip_copy(step):
        return pltpu.make_async_remote_copy(
            src_ref=mine.at[step],
            dst_ref=chip_in.at[step],
            send_sem=csend.at[step],
            recv_sem=crecv.at[step],
            device_id=(ctx, ((x + step) % chips) * 2 + core),
            device_id_type=MESH,
        )

    order = sorted(range(chips), key=lambda s: -min(s, chips - s))
    for step in order:
        pair_out[step] = columns((x + step) % chips, 1 - core)
    pl.semaphore_wait(barrier, chips)
    for step in order:
        pair_copy(step).start()
    for step in order:
        mine[step] = columns((x + step) % chips, core)
    for step in order:
        pair_copy(step).wait_recv()
        mine[step] = mine[step] + pair_in[step]
        if step:
            chip_copy(step).start()
    total = mine[0]
    for step in order[1:-1] + order[:-1][:1]:
        chip_copy(step).wait_recv()
        total = total + chip_in[step]
    out_ref[...] = total.astype(BF16)
    for step in order:
        pair_copy(step).wait_send()
        if step:
            chip_copy(step).wait_send()


def per_device(
    queries, key_rows, value_rows, beta_logit, log_decay, out_gate, norm_gain, out_weight
):
    heads = value_rows.shape[1] // D
    tokens = value_rows.shape[0]
    nz = 2 * heads
    ny = lax.axis_size("ctx") // nz
    n = lax.axis_size("head")
    width = out_weight.shape[1] // n
    vmem = pl.BlockSpec(memory_space=pltpu.VMEM)
    dma = pltpu.SemaphoreType.DMA
    gated = pl.pallas_call(
        functools.partial(ctx_kernel, ny, nz),
        out_shape=jax.ShapeDtypeStruct(value_rows.shape, BF16),
        in_specs=[vmem] * 7,
        out_specs=vmem,
        scratch_shapes=[
            pltpu.VMEM((heads, D, 2 * D), F32),
            pltpu.VMEM((nz, D, 2 * D), F32),
            pltpu.VMEM((ny, D, 2 * D), F32),
            pltpu.VMEM((D, 2 * D), F32),
            pltpu.VMEM((nz, D, 2 * D), F32),
            pltpu.VMEM((nz, D, D), F32),
            pltpu.VMEM((heads, D, D), F32),
            pltpu.VMEM((heads, D, D), F32),
            pltpu.VMEM((heads, D, D), F32),
            pltpu.VMEM((D, D), F32),
            dma((heads,)),
            dma((nz,)),
            dma((ny,)),
            dma((ny,)),
            dma((nz,)),
            dma((heads,)),
        ],
        compiler_params=pltpu.CompilerParams(
            collective_id=0, has_side_effects=True, vmem_limit_bytes=48 * 2**20
        ),
        name="ctx_scan",
    )(
        queries,
        key_rows,
        value_rows,
        beta_logit.T,
        log_decay.T,
        out_gate,
        norm_gain[None],
    )
    return pl.pallas_call(
        functools.partial(head_kernel, n),
        out_shape=jax.ShapeDtypeStruct((tokens, width), BF16),
        in_specs=[vmem] * 2,
        out_specs=vmem,
        scratch_shapes=[
            pltpu.VMEM((n // 2, tokens, width), F32),
            pltpu.VMEM((n // 2, tokens, width), F32),
            pltpu.VMEM((n // 2, tokens, width), F32),
            pltpu.VMEM((n // 2, tokens, width), F32),
            dma((n // 2,)),
            dma((n // 2,)),
            dma((n // 2,)),
            dma((n // 2,)),
        ],
        compiler_params=pltpu.CompilerParams(
            collective_id=1, has_side_effects=True, vmem_limit_bytes=48 * 2**20
        ),
        name="head_sum",
    )(gated, out_weight)


def solution(mesh):
    return jax.shard_map(
        per_device,
        mesh=mesh,
        in_specs=(
            P("ctx", "head"),
            P("ctx", "head"),
            P("ctx", "head"),
            P("ctx", "head"),
            P("ctx", "head"),
            P("ctx", "head"),
            P(),
            P("head", None),
        ),
        out_specs=P("ctx", "head"),
        check_vma=False,
    )
```

time: 506 us -> 70.6 us (0.14)
  the two profiles are of different devices: /device:TPU:57 before, /device:TPU:49 now
where the time goes in v1:
time: 70.6 us; the launch traced here: 70.2 us
  Pallas kernels  62.5 us (89%)
  local copies, waits for them, and re-layouts  7.72 us (11%)
    pallas_call x1, Pallas kernels, per_device(): pl.pallas_call(functools.partial(ctx_kernel, ny, nz), out_shape=jax.Shape...  45.5 us
    pallas_call x1, Pallas kernels, per_device(): pl.pallas_call(functools.partial(head_kernel, n), out_shape=jax.ShapeDtyp...  17 us
    unnamed x17, local copies, waits for them, and re-layouts  7.72 us

profile of v1, /device:TPU:49, one launch (start us, length us, event | category | flops | bytes accessed | tf_op | source)
XLA Modules:
  0.0 70.2 jit_solution(14534150651678232996)
XLA Ops:
  0.0 0.0 copy-start.1
  0.0 0.9 %copy-done.1 = bf16[128,512]{1,0:T(8,128)(2,1)S(1)} copy-done((bf16[128,512]{1,0:T(8,128)(2,1)S(1)}, bf16[128,512]{1,0:T(8,128)(2,1)}, u32[]{:S(2)}) %copy-start.1) | copy-done | bytes 131096
  0.9 0.0 copy-start.2
  0.9 0.9 %copy-done.2 = bf16[128,512]{1,0:T(8,128)(2,1)S(1)} copy-done((bf16[128,512]{1,0:T(8,128)(2,1)S(1)}, bf16[128,512]{1,0:T(8,128)(2,1)}, u32[]{:S(2)}) %copy-start.2) | copy-done | bytes 131096
  1.8 0.0 copy-start.3
  1.8 0.8 %copy-done.3 = bf16[128,256]{1,0:T(8,128)(2,1)S(1)} copy-done((bf16[128,256]{1,0:T(8,128)(2,1)S(1)}, bf16[128,256]{1,0:T(8,128)(2,1)}, u32[]{:S(2)}) %copy-start.3) | copy-done | bytes 65560
  2.6 0.0 copy-start.4
  2.7 0.8 %copy-done.4 = bf16[128,256]{1,0:T(8,128)(2,1)S(1)} copy-done((bf16[128,256]{1,0:T(8,128)(2,1)S(1)}, bf16[128,256]{1,0:T(8,128)(2,1)}, u32[]{:S(2)}) %copy-start.4) | copy-done | bytes 65560
  3.5 0.0 copy-start.5
  3.5 0.7 copy-done.5
  4.2 0.0 copy-start.6
  4.2 0.7 copy-done.6
  4.9 0.0 copy-start.7
  4.9 0.7 copy-done.7
  5.5 45.5 %ctx_scan.1.gated_ref = bf16[128,512]{1,0:T(8,128)(2,1)S(1)} custom-call(bf16[128,256]{1,0:T(8,128)(2,1)S(1)} %copy-done.3, bf16[128,256]{1,0:T(8,128)(2,1)S(1)} %copy-done.4, bf16[128,512]{1,0:T(8,128)(2,1)S(1)} %copy-done.1, f32[4,128]{1,0:T(4,128)S(1)} %bitcast.3, f32[4,128]{1,0:T(4,128)S(1)} %bitcast.4, bf16[128,512]{1,0:T(8,128)(2,1)S(1)} %copy-done.2, ...), custom_call_target="tpu_custom_call" | custom-call | tf_op jit(solution)/shard_map/ctx_scan/pallas_call | solution.py:401
  51.0 0.0 copy-start
  51.0 1.6 %copy-done = bf16[512,2048]{1,0:T(8,128)(2,1)S(1)} copy-done((bf16[512,2048]{1,0:T(8,128)(2,1)S(1)}, bf16[512,2048]{1,0:T(8,128)(2,1)}, u32[]{:S(2)}) %copy-start) | copy-done | bytes 2097176
  52.6 17.0 %head_sum.1 = bf16[128,256]{1,0:T(8,128)(2,1)S(1)} custom-call(bf16[128,512]{1,0:T(8,128)(2,1)S(1)} %ctx_scan.1.gated_ref, bf16[512,2048]{1,0:T(8,128)(2,1)S(1)} %copy-done), custom_call_target="tpu_custom_call" | custom-call | tf_op jit(solution)/shard_map/head_sum/pallas_call | solution.py:437
  69.6 0.6 copy.10
Async XLA Ops:
  0.0 0.9 %copy-start.1 = (bf16[128,512]{1,0:T(8,128)(2,1)S(1)}, bf16[128,512]{1,0:T(8,128)(2,1)}, u32[]{:S(2)}) copy-start(bf16[128,512]{1,0:T(8,128)(2,1)} %v_ref.1) | copy-start | bytes 393220
  0.9 0.9 %copy-start.2 = (bf16[128,512]{1,0:T(8,128)(2,1)S(1)}, bf16[128,512]{1,0:T(8,128)(2,1)}, u32[]{:S(2)}) copy-start(bf16[128,512]{1,0:T(8,128)(2,1)} %gate_ref.1) | copy-start | bytes 393220
  1.8 0.8 %copy-start.3 = (bf16[128,256]{1,0:T(8,128)(2,1)S(1)}, bf16[128,256]{1,0:T(8,128)(2,1)}, u32[]{:S(2)}) copy-start(bf16[128,256]{1,0:T(8,128)(2,1)} %q_ref.1) | copy-start | bytes 196612
  2.6 0.8 %copy-start.4 = (bf16[128,256]{1,0:T(8,128)(2,1)S(1)}, bf16[128,256]{1,0:T(8,128)(2,1)}, u32[]{:S(2)}) copy-start(bf16[128,256]{1,0:T(8,128)(2,1)} %k_ref.1) | copy-start | bytes 196612
  3.5 0.7 copy-start.5
  4.2 0.7 copy-start.6
  4.9 0.7 copy-start.7
  51.0 1.6 %copy-start = (bf16[512,2048]{1,0:T(8,128)(2,1)S(1)}, bf16[512,2048]{1,0:T(8,128)(2,1)}, u32[]{:S(2)}) copy-start(bf16[512,2048]{1,0:T(8,128)(2,1)} %weight_ref.1) | copy-start | bytes 6291460

commit v2 on v1

v2 whole, which is shorter than its diff:
```python
import functools

import jax
import jax.numpy as jnp
from jax import lax
from jax.experimental import pallas as pl
from jax.experimental.pallas import tpu as pltpu
from jax.sharding import PartitionSpec as P

MESH = pl.DeviceIdType.MESH
F32 = jnp.float32
BF16 = jnp.bfloat16
D = 128


def mm(a, b):
    batch = tuple(range(a.ndim - 2))
    dims = (((a.ndim - 1,), (b.ndim - 2,)), (batch, batch))
    return lax.dot_general(a, b, dims, precision=lax.Precision.HIGHEST, preferred_element_type=F32)


def mm_bf16(a, b):
    batch = tuple(range(a.ndim - 2))
    dims = (((a.ndim - 1,), (b.ndim - 2,)), (batch, batch))
    return lax.dot_general(a, b, dims, preferred_element_type=F32)


def mm_split(a, b):
    high = a.astype(BF16)
    low = (a - high.astype(F32)).astype(BF16)
    return mm_bf16(high, b) + mm_bf16(low, b)


def cut(a):
    high = a.astype(BF16)
    return high, (a - high.astype(F32)).astype(BF16)


def mm3(a, b):
    a_high, a_low = cut(a)
    b_high, b_low = cut(b)
    return mm_bf16(a_high, b_high) + (mm_bf16(a_high, b_low) + mm_bf16(a_low, b_high))


def nt(a, b):
    return lax.dot_general(
        a, b, (((1,), (1,)), ((), ())), precision=lax.Precision.HIGHEST, preferred_element_type=F32
    )


def iotas(n):
    return (
        lax.broadcasted_iota(jnp.int32, (n, n), 0),
        lax.broadcasted_iota(jnp.int32, (n, n), 1),
    )


def unit_lower_inverse(strict_part):
    row, col = iotas(D)
    eye = jnp.where(row == col, 1.0, 0.0).astype(F32)

    def off(half):
        shift = half.bit_length() - 1
        rb, cb = row >> shift, col >> shift
        mask = ((rb ^ cb) == 1) & (rb > cb)
        return jnp.where(mask[None], strict_part, 0.0)

    inverse = eye[None] - off(1)
    half = 2
    while half < D:
        inverse = inverse - mm(inverse, mm(off(half), inverse))
        half *= 2
    return inverse


def follow(out, later, earlier):
    both = mm3(later[0], jnp.concatenate([earlier[0], earlier[1]], axis=1))
    out[0] = both[:, :D]
    out[1] = both[:, D:] + later[1]


def kernel(
    ny,
    nz,
    n,
    q_hbm,
    k_hbm,
    v_hbm,
    beta_hbm,
    decay_hbm,
    gate_hbm,
    gain_hbm,
    weight_hbm,
    out_ref,
    q_ref,
    k_ref,
    v_ref,
    beta_ref,
    decay_ref,
    gate_ref,
    gain_ref,
    weight_ref,
    own,
    zin,
    yin,
    total_ref,
    tree,
    prefix,
    sout,
    sin,
    within,
    qmap,
    state_ref,
    gated_ref,
    pair_out,
    pair_in,
    mine,
    chip_in,
    load,
    zsend,
    zrecv,
    ysend,
    yrecv,
    rsend,
    rrecv,
    psend,
    precv,
    csend,
    crecv,
):
    heads = v_ref.shape[1] // D
    kheads = k_ref.shape[1] // D
    group = heads // kheads
    chips = n // 2
    width = out_ref.shape[1]
    slots = 2 * nz
    blocks = ny // 2
    ctx, head = lax.axis_index("ctx"), lax.axis_index("head")
    y, z = ctx // nz, ctx % nz
    x, core = head // 2, head % 2
    block, row_in = y // 2, y % 2
    place = row_in * nz + z
    sibling = x * 2 + 1 - core
    worker = (z % 2 == core) & (row_in == core)

    def at(other_block, other_row, other_z):
        return (other_block * 2 + other_row) * nz + other_z

    barrier = pltpu.get_barrier_semaphore()
    greeted = 0

    def greet(where):
        pl.semaphore_signal(barrier, inc=1, device_id=where, device_id_type=MESH)

    for dr in range(2):
        for dz in range(nz):
            if dr or dz:
                greet((at(block, (row_in + dr) % 2, (z + dz) % nz), head))
                greeted += 1
    for db in range(1, blocks):
        greet((at((block + db) % blocks, row_in, z), head))
        greeted += 1
    greet((ctx, sibling))
    for dx in range(1, chips):
        greet((ctx, ((x + dx) % chips) * 2 + core))
    greeted += chips

    loads = [
        pltpu.make_async_copy(src, dst, load.at[i])
        for i, (src, dst) in enumerate(
            [
                (k_hbm, k_ref),
                (decay_hbm, decay_ref),
                (beta_hbm, beta_ref),
                (v_hbm, v_ref),
                (q_hbm, q_ref),
                (gate_hbm, gate_ref),
                (gain_hbm, gain_ref),
                (weight_hbm, weight_ref),
            ]
        )
    ]
    for copy in loads:
        copy.start()
    for copy in loads[:5]:
        copy.wait()

    row, col = iotas(D)
    causal, strict = row >= col, row > col
    eye = jnp.where(row == col, 1.0, 0.0).astype(F32)
    tri = jnp.where(causal, 1.0, 0.0).astype(F32)
    keys = jnp.stack([k_ref[:, i * D : (i + 1) * D] for i in range(kheads)])
    queries = jnp.stack([q_ref[:, i * D : (i + 1) * D] for i in range(kheads)])
    values = jnp.stack([v_ref[:, i * D : (i + 1) * D] for i in range(heads)])
    keys32 = keys.astype(F32)
    keys_t32 = jnp.stack([keys32[i].T for i in range(kheads)])
    keys_t = keys_t32.astype(BF16)
    r_col = lax.rsqrt(jnp.sum(keys32 * keys32, axis=2, keepdims=True) + 1e-06)
    r_row = lax.rsqrt(jnp.sum(keys_t32 * keys_t32, axis=1, keepdims=True) + 1e-06)
    gram = mm_bf16(keys, keys_t) * (r_col * r_row)
    scores = mm_bf16(queries, keys_t) * r_row

    beta_row = jax.nn.sigmoid(beta_ref[...])
    decay_row = decay_ref[...]
    cum_row = nt(decay_row, tri)
    cum_col = nt(tri, decay_row)
    beta_col = nt(eye, beta_row)
    exp_row = jnp.exp(cum_row)
    exp_col = jnp.exp(cum_col)
    total = cum_row[:, D - 1 : D]
    exp_total = jnp.exp(total)
    tail_row = jnp.exp(total - cum_row)

    def per_head(fn):
        return jnp.stack([fn(h) for h in range(heads)])

    decay_mat = per_head(
        lambda h: jnp.exp(
            jnp.where(causal, cum_col[:, h : h + 1] - cum_row[h : h + 1, :], -1e30)
        )
    )
    strict_part = per_head(
        lambda h: jnp.where(
            strict, beta_col[:, h : h + 1] * gram[h // group] * decay_mat[h], 0.0
        )
    )
    inverse = unit_lower_inverse(strict_part)
    scaled = per_head(lambda h: inverse[h] * beta_row[h : h + 1, :])
    pseudo = mm_split(scaled, values)
    wy = mm_split(
        per_head(lambda h: scaled[h] * (exp_row[h : h + 1, :] * r_row[h // group])),
        per_head(lambda h: keys[h // group]),
    )
    wy_pseudo = jnp.concatenate([wy, pseudo], axis=2)
    tails = per_head(
        lambda h: keys_t32[h // group] * (r_row[h // group] * tail_row[h : h + 1, :])
    )
    moved = mm(tails, wy_pseudo)
    for h in range(heads):
        own[h, 0] = exp_total[h : h + 1, :] * eye - moved[h, :, :D]
        own[h, 1] = moved[h, :, D:]

    pl.semaphore_wait(barrier, greeted)

    def head_copy(k):
        h = (z // 2 + k) % heads
        return pltpu.make_async_remote_copy(
            src_ref=own.at[h],
            dst_ref=zin.at[place],
            send_sem=zsend.at[k],
            recv_sem=zrecv.at[place],
            device_id=(at(block, core, 2 * h + core), head),
            device_id_type=MESH,
        )

    by_distance = sorted(range(heads), key=lambda k: -min(k, heads - k))
    for k in by_distance:
        if k:
            head_copy(k).start()
        else:

            @pl.when(jnp.logical_not(worker))
            def _():
                head_copy(0).start()

            @pl.when(worker)
            def _():
                zin[pl.ds(place, 1)] = own[pl.ds(z // 2, 1)]

    mixed = mm3(per_head(lambda h: scores[h // group] * decay_mat[h]), wy_pseudo)
    for h in range(heads):
        within[h] = mixed[h, :, D:]
        qmap[h] = exp_col[:, h : h + 1] * queries[h // group].astype(F32) - mixed[h, :, :D]
    for copy in loads[5:]:
        copy.wait()

    def block_copy(target, state_only):
        src = total_ref.at[1] if state_only else total_ref
        dst = yin.at[block, 1] if state_only else yin.at[block]
        return pltpu.make_async_remote_copy(
            src_ref=src,
            dst_ref=dst,
            send_sem=ysend.at[target],
            recv_sem=yrecv.at[block],
            device_id=(at(target, row_in, z), head),
            device_id_type=MESH,
        )

    def each_block_copy(act):
        for target in range(blocks - 1, 0, -1):

            @pl.when(block == 0)
            def _():
                act(block_copy(target, True))

            @pl.when((block > 0) & (target > block))
            def _():
                act(block_copy(target, False))

    def state_copy(dr, dz):
        i = ((row_in + dr) % 2) * nz + (z + dz) % nz
        return pltpu.make_async_remote_copy(
            src_ref=sout.at[i],
            dst_ref=sin.at[z // 2],
            send_sem=rsend.at[dr * nz + dz],
            recv_sem=rrecv.at[z // 2],
            device_id=(at(block, (row_in + dr) % 2, (z + dz) % nz), head),
            device_id_type=MESH,
        )

    def arrived(dst, sem):
        pltpu.make_async_remote_copy(
            src_ref=dst,
            dst_ref=dst,
            send_sem=zsend.at[0],
            recv_sem=sem,
            device_id=(ctx, sibling),
            device_id_type=MESH,
        ).wait_recv()

    targets = [
        (dr, dz)
        for dz in sorted(range(nz), key=lambda d: -min(d, nz - d))
        for dr in (1, 0)
    ]

    @pl.when(worker)
    def _():
        node = {}
        used = 0

        def spot(low, high):
            nonlocal used
            if high - low == 1:
                return zin.at[low]
            if (low, high) == (0, slots):
                return total_ref
            if low == 0:
                return prefix.at[high]
            used += 1
            return tree.at[used - 1]

        for i in range(slots):

            @pl.when(place != i)
            def _():
                arrived(zin.at[i], zrecv.at[i])

            node[(i, i + 1)] = spot(i, i + 1)
            if i == 0:
                prefix[1] = zin[0]
            low, high, span = i, i + 1, 1
            while high % (2 * span) == 0 and 2 * span <= slots:
                out = spot(high - 2 * span, high)
                follow(out, node[(low, high)], node[(low - span, low)])
                low, span = low - span, 2 * span
                node[(low, high)] = out
        each_block_copy(lambda copy: copy.start())
        prefix[0, 0] = eye
        prefix[0, 1] = jnp.zeros((D, D), F32)
        for i in range(3, slots):
            step = i & -i
            if step != i:
                follow(prefix.at[i], node[(i - step, i)], prefix.at[i - step])

        @pl.when(block == 0)
        def _():
            state_ref[...] = jnp.zeros((D, D), F32)

        @pl.when(block > 0)
        def _():
            arrived(yin.at[0, 1], yrecv.at[0])
            state_ref[...] = yin[0, 1]

        for i in range(1, blocks - 1):

            @pl.when(i < block)
            def _():
                arrived(yin.at[i], yrecv.at[i])
                state_ref[...] = mm3(yin[i, 0], state_ref[...]) + yin[i, 1]

        state = state_ref[...]
        for dr, dz in targets:
            i = ((row_in + dr) % 2) * nz + (z + dz) % nz
            block_in = prefix[pl.ds(i, 1)][0]
            result = mm3(block_in[0], state) + block_in[1]
            if dr or dz:
                sout[pl.ds(i, 1)] = result[None]
                state_copy(dr, dz).start()
            else:
                sin[pl.ds(z // 2, 1)] = result[None]

    for h in range(heads):

        @pl.when(jnp.logical_not(worker) | (z // 2 != h))
        def _():
            arrived(sin.at[h], rrecv.at[h])

        core_out = within[h] + mm3(qmap[h], sin[h])
        normed = core_out * lax.rsqrt(jnp.mean(core_out * core_out, axis=1, keepdims=True) + 1e-06)
        gate = gate_ref[:, h * D : (h + 1) * D].astype(F32)
        gated_ref[:, h * D : (h + 1) * D] = (
            normed * gain_ref[...] * (gate / (1.0 + jnp.exp(-gate)))
        ).astype(BF16)

    gated = gated_ref[...]

    def columns(chip, which):
        start = pl.multiple_of((chip * 2 + which) * width, width)
        return mm_bf16(gated, weight_ref[:, pl.ds(start, width)])

    def pair_copy(step):
        return pltpu.make_async_remote_copy(
            src_ref=pair_out.at[step],
            dst_ref=pair_in.at[step],
            send_sem=psend.at[step],
            recv_sem=precv.at[step],
            device_id=(ctx, sibling),
            device_id_type=MESH,
        )

    def chip_copy(step):
        return pltpu.make_async_remote_copy(
            src_ref=mine.at[step],
            dst_ref=chip_in.at[step],
            send_sem=csend.at[step],
            recv_sem=crecv.at[step],
            device_id=(ctx, ((x + step) % chips) * 2 + core),
            device_id_type=MESH,
        )

    order = sorted(range(chips), key=lambda s: -min(s, chips - s))
    for step in order:
        pair_out[step] = columns((x + step) % chips, 1 - core)
        pair_copy(step).start()
    for step in order:
        mine[step] = columns((x + step) % chips, core)
    for step in order:
        pair_copy(step).wait_recv()
        mine[step] = mine[step] + pair_in[step]
        if step:
            chip_copy(step).start()
    summed = mine[0]
    for step in order[1:-1] + order[:-1][:1]:
        chip_copy(step).wait_recv()
        summed = summed + chip_in[step]
    out_ref[...] = summed.astype(BF16)

    for k in range(heads):
        if k:
            head_copy(k).wait_send()
        else:

            @pl.when(jnp.logical_not(worker))
            def _():
                head_copy(0).wait_send()

    @pl.when(worker)
    def _():
        each_block_copy(lambda copy: copy.wait_send())
        for dr, dz in targets:
            if dr or dz:
                state_copy(dr, dz).wait_send()

    for step in order:
        pair_copy(step).wait_send()
        if step:
            chip_copy(step).wait_send()


def per_device(
    queries, key_rows, value_rows, beta_logit, log_decay, out_gate, norm_gain, out_weight
):
    heads = value_rows.shape[1] // D
    tokens = value_rows.shape[0]
    nz = 2 * heads
    ny = lax.axis_size("ctx") // nz
    n = lax.axis_size("head")
    width = out_weight.shape[1] // n
    vmem = pltpu.VMEM
    dma = pltpu.SemaphoreType.DMA
    args = (
        queries,
        key_rows,
        value_rows,
        beta_logit.T,
        log_decay.T,
        out_gate,
        norm_gain[None],
        out_weight,
    )
    return pl.pallas_call(
        functools.partial(kernel, ny, nz, n),
        out_shape=jax.ShapeDtypeStruct((tokens, width), BF16),
        in_specs=[pl.BlockSpec(memory_space=pltpu.HBM)] * len(args),
        out_specs=pl.BlockSpec(memory_space=vmem),
        scratch_shapes=[vmem(a.shape, a.dtype) for a in args]
        + [
            vmem((heads, 2, D, D), F32),
            vmem((2 * nz, 2, D, D), F32),
            vmem((ny // 2, 2, D, D), F32),
            vmem((2, D, D), F32),
            vmem((2 * nz, 2, D, D), F32),
            vmem((2 * nz, 2, D, D), F32),
            vmem((2 * nz, D, D), F32),
            vmem((heads, D, D), F32),
            vmem((heads, D, D), F32),
            vmem((heads, D, D), F32),
            vmem((D, D), F32),
            vmem((tokens, heads * D), BF16),
            vmem((n // 2, tokens, width), F32),
            vmem((n // 2, tokens, width), F32),
            vmem((n // 2, tokens, width), F32),
            vmem((n // 2, tokens, width), F32),
            dma((len(args),)),
            dma((heads,)),
            dma((2 * nz,)),
            dma((ny // 2,)),
            dma((ny // 2,)),
            dma((2 * nz,)),
            dma((heads,)),
            dma((n // 2,)),
            dma((n // 2,)),
            dma((n // 2,)),
            dma((n // 2,)),
        ],
        compiler_params=pltpu.CompilerParams(
            collective_id=0, has_side_effects=True, vmem_limit_bytes=56 * 2**20
        ),
        name="delta_layer",
    )(*args)


def solution(mesh):
    return jax.shard_map(
        per_device,
        mesh=mesh,
        in_specs=(
            P("ctx", "head"),
            P("ctx", "head"),
            P("ctx", "head"),
            P("ctx", "head"),
            P("ctx", "head"),
            P("ctx", "head"),
            P(),
            P("head", None),
        ),
        out_specs=P("ctx", "head"),
        check_vma=False,
    )
```

time: 70.6 us -> 69.1 us (0.979)
  the two profiles are of different devices: /device:TPU:49 before, /device:TPU:57 now
where the time goes in v2:
time: 69.1 us; the launch traced here: 68.9 us
  Pallas kernels  67.4 us (98%)
  local copies, waits for them, and re-layouts  1.47 us (2%)
    pallas_call x1, Pallas kernels, per_device(): pl.pallas_call(functools.partial(kernel, ny, nz, n), out_shape=jax.ShapeD...  67.4 us
    unnamed x1, local copies, waits for them, and re-layouts  1.47 us

profile of v2, /device:TPU:57, one launch (start us, length us, event | category | flops | bytes accessed | tf_op | source)
XLA Modules:
  0.0 68.9 jit_solution(1249353391083019702)
XLA Ops:
  0.0 67.4 %delta_layer.1 = bf16[128,256]{1,0:T(8,128)(2,1)} custom-call(bf16[128,256]{1,0:T(8,128)(2,1)} %q_hbm.1, bf16[128,256]{1,0:T(8,128)(2,1)} %k_hbm.1, bf16[128,512]{1,0:T(8,128)(2,1)} %v_hbm.1, f32[4,128]{1,0:T(4,128)} %bitcast.3, f32[4,128]{1,0:T(4,128)} %bitcast.4, bf16[128,512]{1,0:T(8,128)(2,1)} %gate_hbm.1, f32[1,128]{1,0:T(1,128)} %bitcast.5, ...), custom_call_target="tpu_custom_call" | custom-call | tf_op jit(solution)/shard_map/delta_layer/pallas_call | solution.py:492
  67.4 1.5 %copy.10 = bf16[128,256]{1,0:T(8,128)(2,1)} copy(bf16[128,256]{1,0:T(8,128)(2,1)} %delta_layer.1) | data formatting | bytes 131072

commit v3 on v2

--- a/solution.py
+++ b/solution.py
@@ -71,12 +71,6 @@
         inverse = inverse - mm(inverse, mm(off(half), inverse))
         half *= 2
     return inverse
-
-
-def follow(out, later, earlier):
-    both = mm3(later[0], jnp.concatenate([earlier[0], earlier[1]], axis=1))
-    out[0] = both[:, :D]
-    out[1] = both[:, D:] + later[1]
 
 
 def kernel(
@@ -100,27 +94,36 @@
     gate_ref,
     gain_ref,
     weight_ref,
-    own,
-    zin,
-    yin,
-    total_ref,
-    tree,
-    prefix,
+    own_t,
+    own_s,
+    zin_t,
+    zin_s,
+    yin_t,
+    yin_s,
+    total_t,
+    total_s,
+    prefix_t,
+    prefix_s,
+    suffix,
+    reach,
     sout,
     sin,
     within,
     qmap,
-    state_ref,
     gated_ref,
     pair_out,
     pair_in,
     mine,
     chip_in,
     load,
-    zsend,
-    zrecv,
-    ysend,
-    yrecv,
+    zsend_t,
+    zsend_s,
+    zrecv_t,
+    zrecv_s,
+    ysend_t,
+    ysend_s,
+    yrecv_t,
+    yrecv_s,
     rsend,
     rrecv,
     psend,
@@ -133,37 +136,25 @@
     group = heads // kheads
     chips = n // 2
     width = out_ref.shape[1]
-    slots = 2 * nz
-    blocks = ny // 2
     ctx, head = lax.axis_index("ctx"), lax.axis_index("head")
     y, z = ctx // nz, ctx % nz
     x, core = head // 2, head % 2
-    block, row_in = y // 2, y % 2
-    place = row_in * nz + z
     sibling = x * 2 + 1 - core
-    worker = (z % 2 == core) & (row_in == core)
-
-    def at(other_block, other_row, other_z):
-        return (other_block * 2 + other_row) * nz + other_z
+    worker = z % 2 == core
 
     barrier = pltpu.get_barrier_semaphore()
-    greeted = 0
 
     def greet(where):
         pl.semaphore_signal(barrier, inc=1, device_id=where, device_id_type=MESH)
 
-    for dr in range(2):
-        for dz in range(nz):
-            if dr or dz:
-                greet((at(block, (row_in + dr) % 2, (z + dz) % nz), head))
-                greeted += 1
-    for db in range(1, blocks):
-        greet((at((block + db) % blocks, row_in, z), head))
-        greeted += 1
+    for dz in range(1, nz):
+        greet((y * nz + (z + dz) % nz, head))
+    for dy in range(1, ny):
+        greet((((y + dy) % ny) * nz + z, head))
     greet((ctx, sibling))
     for dx in range(1, chips):
         greet((ctx, ((x + dx) % chips) * 2 + core))
-    greeted += chips
+    greeted = nz - 1 + ny - 1 + chips
 
     loads = [
         pltpu.make_async_copy(src, dst, load.at[i])
@@ -237,35 +228,37 @@
     )
     moved = mm(tails, wy_pseudo)
     for h in range(heads):
-        own[h, 0] = exp_total[h : h + 1, :] * eye - moved[h, :, :D]
-        own[h, 1] = moved[h, :, D:]
+        own_t[h] = exp_total[h : h + 1, :] * eye - moved[h, :, :D]
+        own_s[h] = moved[h, :, D:]
 
     pl.semaphore_wait(barrier, greeted)
 
-    def head_copy(k):
+    def head_copy(k, own, zin, send, recv):
         h = (z // 2 + k) % heads
         return pltpu.make_async_remote_copy(
             src_ref=own.at[h],
-            dst_ref=zin.at[place],
-            send_sem=zsend.at[k],
-            recv_sem=zrecv.at[place],
-            device_id=(at(block, core, 2 * h + core), head),
+            dst_ref=zin.at[z],
+            send_sem=send.at[k],
+            recv_sem=recv.at[z],
+            device_id=(y * nz + 2 * h + core, head),
             device_id_type=MESH,
         )
 
+    moves = ((own_t, zin_t, zsend_t, zrecv_t), (own_s, zin_s, zsend_s, zrecv_s))
     by_distance = sorted(range(heads), key=lambda k: -min(k, heads - k))
-    for k in by_distance:
-        if k:
-            head_copy(k).start()
-        else:
-
-            @pl.when(jnp.logical_not(worker))
-            def _():
-                head_copy(0).start()
-
-            @pl.when(worker)
-            def _():
-                zin[pl.ds(place, 1)] = own[pl.ds(z // 2, 1)]
+    for move in moves:
+        for k in by_distance:
+            if k:
+                head_copy(k, *move).start()
+            else:
+
+                @pl.when(jnp.logical_not(worker))
+                def _():
+                    head_copy(0, *move).start()
+
+                @pl.when(worker)
+                def _():
+                    move[1][pl.ds(z, 1)] = move[0][pl.ds(z // 2, 1)]
 
     mixed = mm3(per_head(lambda h: scores[h // group] * decay_mat[h]), wy_pseudo)
     for h in range(heads):
@@ -274,37 +267,40 @@
     for copy in loads[5:]:
         copy.wait()
 
-    def block_copy(target, state_only):
-        src = total_ref.at[1] if state_only else total_ref
-        dst = yin.at[block, 1] if state_only else yin.at[block]
+    def row_copy(dy, src, yin, send, recv):
         return pltpu.make_async_remote_copy(
             src_ref=src,
-            dst_ref=dst,
-            send_sem=ysend.at[target],
-            recv_sem=yrecv.at[block],
-            device_id=(at(target, row_in, z), head),
+            dst_ref=yin.at[dy],
+            send_sem=send.at[dy],
+            recv_sem=recv.at[dy],
+            device_id=((y + dy) * nz + z, head),
             device_id_type=MESH,
         )
 
-    def each_block_copy(act):
-        for target in range(blocks - 1, 0, -1):
-
-            @pl.when(block == 0)
+    far_rows = sorted(range(1, ny), key=lambda d: -min(d, ny - d))
+
+    def each_row_t(act):
+        for dy in far_rows:
+
+            @pl.when((y > 0) & (y + dy < ny))
             def _():
-                act(block_copy(target, True))
-
-            @pl.when((block > 0) & (target > block))
+                act(row_copy(dy, total_t, yin_t, ysend_t, yrecv_t))
+
+    def each_row_s(act):
+        for dy in far_rows:
+
+            @pl.when(y + dy < ny)
             def _():
-                act(block_copy(target, False))
-
-    def state_copy(dr, dz):
-        i = ((row_in + dr) % 2) * nz + (z + dz) % nz
+                act(row_copy(dy, total_s, yin_s, ysend_s, yrecv_s))
+
+    def state_copy(dz):
+        i = (z + dz) % nz
         return pltpu.make_async_remote_copy(
             src_ref=sout.at[i],
             dst_ref=sin.at[z // 2],
-            send_sem=rsend.at[dr * nz + dz],
+            send_sem=rsend.at[dz],
             recv_sem=rrecv.at[z // 2],
-            device_id=(at(block, (row_in + dr) % 2, (z + dz) % nz), head),
+            device_id=(y * nz + i, head),
             device_id_type=MESH,
         )
 
@@ -312,81 +308,96 @@
         pltpu.make_async_remote_copy(
             src_ref=dst,
             dst_ref=dst,
-            send_sem=zsend.at[0],
+            send_sem=zsend_t.at[0],
             recv_sem=sem,
             device_id=(ctx, sibling),
             device_id_type=MESH,
         ).wait_recv()
 
-    targets = [
-        (dr, dz)
-        for dz in sorted(range(nz), key=lambda d: -min(d, nz - d))
-        for dr in (1, 0)
-    ]
+    targets = sorted(range(nz), key=lambda d: -min(d, nz - d))
 
     @pl.when(worker)
     def _():
-        node = {}
-        used = 0
-
-        def spot(low, high):
-            nonlocal used
-            if high - low == 1:
-                return zin.at[low]
-            if (low, high) == (0, slots):
-                return total_ref
-            if low == 0:
-                return prefix.at[high]
-            used += 1
-            return tree.at[used - 1]
-
-        for i in range(slots):
-
-            @pl.when(place != i)
+        def wait_place(zin, recv):
+            for i in range(nz):
+
+                @pl.when(z != i)
+                def _():
+                    arrived(zin.at[i], recv.at[i])
+
+        wait_place(zin_t, zrecv_t)
+        first = {(i, i + 1): zin_t[i] for i in range(nz)}
+
+        def trans(low, high):
+            if (low, high) not in first:
+                span = 1 << ((high - low - 1).bit_length() - 1)
+                middle = low + span if low % (2 * span) == 0 else high - span
+                first[(low, high)] = mm3(trans(middle, high), trans(low, middle))
+            return first[(low, high)]
+
+        total_t[...] = trans(0, nz)
+        each_row_t(lambda copy: copy.start())
+        for i in range(1, nz):
+            suffix[:, (i - 1) * D : i * D] = trans(i, nz)
+        prefix_t[0] = eye
+        for i in range(1, nz):
+            prefix_t[i] = trans(0, i)
+
+        wait_place(zin_s, zrecv_s)
+        total_s[...] = zin_s[nz - 1] + mm3(
+            suffix[...], zin_s[: nz - 1].reshape((nz - 1) * D, D)
+        )
+        each_row_s(lambda copy: copy.start())
+
+        prefix_s[0] = jnp.zeros((D, D), F32)
+        states = {(i, i + 1): zin_s[i] for i in range(nz)}
+
+        def state_of(low, high):
+            if (low, high) not in states:
+                span = 1 << ((high - low - 1).bit_length() - 1)
+                middle = low + span if low % (2 * span) == 0 else high - span
+                states[(low, high)] = mm3(trans(middle, high), state_of(low, middle)) + state_of(
+                    middle, high
+                )
+            return states[(low, high)]
+
+        for i in range(1, nz):
+            prefix_s[i] = state_of(0, i)
+
+        reach[:, :D] = eye
+        for dy in range(2, ny):
+            here = slice((dy - 1) * D, dy * D)
+            before = slice((dy - 2) * D, (dy - 1) * D)
+
+            @pl.when(dy <= y)
             def _():
-                arrived(zin.at[i], zrecv.at[i])
-
-            node[(i, i + 1)] = spot(i, i + 1)
-            if i == 0:
-                prefix[1] = zin[0]
-            low, high, span = i, i + 1, 1
-            while high % (2 * span) == 0 and 2 * span <= slots:
-                out = spot(high - 2 * span, high)
-                follow(out, node[(low, high)], node[(low - span, low)])
-                low, span = low - span, 2 * span
-                node[(low, high)] = out
-        each_block_copy(lambda copy: copy.start())
-        prefix[0, 0] = eye
-        prefix[0, 1] = jnp.zeros((D, D), F32)
-        for i in range(3, slots):
-            step = i & -i
-            if step != i:
-                follow(prefix.at[i], node[(i - step, i)], prefix.at[i - step])
-
-        @pl.when(block == 0)
-        def _():
-            state_ref[...] = jnp.zeros((D, D), F32)
-
-        @pl.when(block > 0)
-        def _():
-            arrived(yin.at[0, 1], yrecv.at[0])
-            state_ref[...] = yin[0, 1]
-
-        for i in range(1, blocks - 1):
-
-            @pl.when(i < block)
+                arrived(yin_t.at[dy - 1], yrecv_t.at[dy - 1])
+                if dy == 2:
+                    reach[:, here] = yin_t[1]
+                else:
+                    reach[:, here] = mm3(reach[:, before], yin_t[dy - 1])
+
+            @pl.when(dy > y)
             def _():
-                arrived(yin.at[i], yrecv.at[i])
-                state_ref[...] = mm3(yin[i, 0], state_ref[...]) + yin[i, 1]
-
-        state = state_ref[...]
-        for dr, dz in targets:
-            i = ((row_in + dr) % 2) * nz + (z + dz) % nz
-            block_in = prefix[pl.ds(i, 1)][0]
-            result = mm3(block_in[0], state) + block_in[1]
-            if dr or dz:
+                reach[:, here] = jnp.zeros((D, D), F32)
+
+        for dy in range(1, ny):
+
+            @pl.when(dy <= y)
+            def _():
+                arrived(yin_s.at[dy], yrecv_s.at[dy])
+
+            @pl.when(dy > y)
+            def _():
+                yin_s[dy] = jnp.zeros((D, D), F32)
+
+        state = mm3(reach[...], yin_s[1:].reshape((ny - 1) * D, D))
+        for dz in targets:
+            i = (z + dz) % nz
+            result = mm3(prefix_t[pl.ds(i, 1)][0], state) + prefix_s[pl.ds(i, 1)][0]
+            if dz:
                 sout[pl.ds(i, 1)] = result[None]
-                state_copy(dr, dz).start()
+                state_copy(dz).start()
             else:
                 sin[pl.ds(z // 2, 1)] = result[None]
 
@@ -446,21 +457,23 @@
         summed = summed + chip_in[step]
     out_ref[...] = summed.astype(BF16)
 
-    for k in range(heads):
-        if k:
-            head_copy(k).wait_send()
-        else:
-
-            @pl.when(jnp.logical_not(worker))
-            def _():
-                head_copy(0).wait_send()
+    for move in moves:
+        for k in range(heads):
+            if k:
+                head_copy(k, *move).wait_send()
+            else:
+
+                @pl.when(jnp.logical_not(worker))
+                def _():
+                    head_copy(0, *move).wait_send()
 
     @pl.when(worker)
     def _():
-        each_block_copy(lambda copy: copy.wait_send())
-        for dr, dz in targets:
-            if dr or dz:
-                state_copy(dr, dz).wait_send()
+        each_row_t(lambda copy: copy.wait_send())
+        each_row_s(lambda copy: copy.wait_send())
+        for dz in targets:
+            if dz:
+                state_copy(dz).wait_send()
 
     for step in order:
         pair_copy(step).wait_send()
@@ -496,17 +509,22 @@
         out_specs=pl.BlockSpec(memory_space=vmem),
         scratch_shapes=[vmem(a.shape, a.dtype) for a in args]
         + [
-            vmem((heads, 2, D, D), F32),
-            vmem((2 * nz, 2, D, D), F32),
-            vmem((ny // 2, 2, D, D), F32),
-            vmem((2, D, D), F32),
-            vmem((2 * nz, 2, D, D), F32),
-            vmem((2 * nz, 2, D, D), F32),
-            vmem((2 * nz, D, D), F32),
+            vmem((heads, D, D), F32),
+            vmem((heads, D, D), F32),
+            vmem((nz, D, D), F32),
+            vmem((nz, D, D), F32),
+            vmem((ny, D, D), F32),
+            vmem((ny, D, D), F32),
+            vmem((D, D), F32),
+            vmem((D, D), F32),
+            vmem((nz, D, D), F32),
+            vmem((nz, D, D), F32),
+            vmem((D, (nz - 1) * D), F32),
+            vmem((D, (ny - 1) * D), F32),
+            vmem((nz, D, D), F32),
             vmem((heads, D, D), F32),
             vmem((heads, D, D), F32),
             vmem((heads, D, D), F32),
-            vmem((D, D), F32),
             vmem((tokens, heads * D), BF16),
             vmem((n // 2, tokens, width), F32),
             vmem((n // 2, tokens, width), F32),
@@ -514,10 +532,14 @@
             vmem((n // 2, tokens, width), F32),
             dma((len(args),)),
             dma((heads,)),
-            dma((2 * nz,)),
-            dma((ny // 2,)),
-            dma((ny // 2,)),
-            dma((2 * nz,)),
+            dma((heads,)),
+            dma((nz,)),
+            dma((nz,)),
+            dma((ny,)),
+            dma((ny,)),
+            dma((ny,)),
+            dma((ny,)),
+            dma((nz,)),
             dma((heads,)),
             dma((n // 2,)),
             dma((n // 2,)),

time: 69.1 us -> 58.8 us (0.85)
  the two profiles are of different devices: /device:TPU:57 before, /device:TPU:41 now
where the time goes in v3:
time: 58.8 us; the launch traced here: 58.7 us
  Pallas kernels  57.2 us (97%)
  local copies, waits for them, and re-layouts  1.47 us (2%)
    pallas_call x1, Pallas kernels, per_device(): pl.pallas_call(functools.partial(kernel, ny, nz, n), out_shape=jax.ShapeD...  57.2 us
    unnamed x1, local copies, waits for them, and re-layouts  1.47 us

profile of v3, /device:TPU:41, one launch (start us, length us, event | category | flops | bytes accessed | tf_op | source)
XLA Modules:
  0.0 58.7 jit_solution(2193587070957024926)
XLA Ops:
  0.0 57.2 %delta_layer.1 = bf16[128,256]{1,0:T(8,128)(2,1)} custom-call(bf16[128,256]{1,0:T(8,128)(2,1)} %q_hbm.1, bf16[128,256]{1,0:T(8,128)(2,1)} %k_hbm.1, bf16[128,512]{1,0:T(8,128)(2,1)} %v_hbm.1, f32[4,128]{1,0:T(4,128)} %bitcast.3, f32[4,128]{1,0:T(4,128)} %bitcast.4, bf16[128,512]{1,0:T(8,128)(2,1)} %gate_hbm.1, f32[1,128]{1,0:T(1,128)} %bitcast.5, ...), custom_call_target="tpu_custom_call" | custom-call | tf_op jit(solution)/shard_map/delta_layer/pallas_call | solution.py:505
  57.2 1.5 %copy.10 = bf16[128,256]{1,0:T(8,128)(2,1)} copy(bf16[128,256]{1,0:T(8,128)(2,1)} %delta_layer.1) | data formatting | bytes 131072

commit v4 on v3

--- a/solution.py
+++ b/solution.py
@@ -68,7 +68,7 @@
     inverse = eye[None] - off(1)
     half = 2
     while half < D:
-        inverse = inverse - mm(inverse, mm(off(half), inverse))
+        inverse = inverse - mm3(inverse, mm3(off(half), inverse))
         half *= 2
     return inverse
 
@@ -110,11 +110,13 @@
     sin,
     within,
     qmap,
+    gating,
     gated_ref,
     pair_out,
     pair_in,
     mine,
     chip_in,
+    ready,
     load,
     zsend_t,
     zsend_s,
@@ -142,20 +144,6 @@
     sibling = x * 2 + 1 - core
     worker = z % 2 == core
 
-    barrier = pltpu.get_barrier_semaphore()
-
-    def greet(where):
-        pl.semaphore_signal(barrier, inc=1, device_id=where, device_id_type=MESH)
-
-    for dz in range(1, nz):
-        greet((y * nz + (z + dz) % nz, head))
-    for dy in range(1, ny):
-        greet((((y + dy) % ny) * nz + z, head))
-    greet((ctx, sibling))
-    for dx in range(1, chips):
-        greet((ctx, ((x + dx) % chips) * 2 + core))
-    greeted = nz - 1 + ny - 1 + chips
-
     loads = [
         pltpu.make_async_copy(src, dst, load.at[i])
         for i, (src, dst) in enumerate(
@@ -173,7 +161,29 @@
     ]
     for copy in loads:
         copy.start()
-    for copy in loads[:5]:
+
+    barrier = pltpu.get_barrier_semaphore()
+
+    def greet(where):
+        pl.semaphore_signal(barrier, inc=1, device_id=where, device_id_type=MESH)
+
+    for other in range(1, nz):
+
+        @pl.when(other > z)
+        def _():
+            greet((y * nz + other, head))
+
+    for other in range(ny - 1):
+
+        @pl.when(other < y)
+        def _():
+            greet((other * nz + z, head))
+
+    greet((ctx, sibling))
+    for dx in range(1, chips):
+        greet((ctx, ((x + dx) % chips) * 2 + core))
+
+    for copy in loads[:3]:
         copy.wait()
 
     row, col = iotas(D)
@@ -181,15 +191,12 @@
     eye = jnp.where(row == col, 1.0, 0.0).astype(F32)
     tri = jnp.where(causal, 1.0, 0.0).astype(F32)
     keys = jnp.stack([k_ref[:, i * D : (i + 1) * D] for i in range(kheads)])
-    queries = jnp.stack([q_ref[:, i * D : (i + 1) * D] for i in range(kheads)])
-    values = jnp.stack([v_ref[:, i * D : (i + 1) * D] for i in range(heads)])
     keys32 = keys.astype(F32)
     keys_t32 = jnp.stack([keys32[i].T for i in range(kheads)])
     keys_t = keys_t32.astype(BF16)
     r_col = lax.rsqrt(jnp.sum(keys32 * keys32, axis=2, keepdims=True) + 1e-06)
     r_row = lax.rsqrt(jnp.sum(keys_t32 * keys_t32, axis=1, keepdims=True) + 1e-06)
     gram = mm_bf16(keys, keys_t) * (r_col * r_row)
-    scores = mm_bf16(queries, keys_t) * r_row
 
     beta_row = jax.nn.sigmoid(beta_ref[...])
     decay_row = decay_ref[...]
@@ -197,7 +204,6 @@
     cum_col = nt(tri, decay_row)
     beta_col = nt(eye, beta_row)
     exp_row = jnp.exp(cum_row)
-    exp_col = jnp.exp(cum_col)
     total = cum_row[:, D - 1 : D]
     exp_total = jnp.exp(total)
     tail_row = jnp.exp(total - cum_row)
@@ -215,57 +221,88 @@
             strict, beta_col[:, h : h + 1] * gram[h // group] * decay_mat[h], 0.0
         )
     )
+    pl.semaphore_wait(barrier, z + (ny - 1 - y) + chips)
+    for other in range(nz - 1):
+
+        @pl.when(other < z)
+        def _():
+            pl.semaphore_signal(
+                ready.at[z], inc=1, device_id=(y * nz + other, head), device_id_type=MESH
+            )
+
     inverse = unit_lower_inverse(strict_part)
     scaled = per_head(lambda h: inverse[h] * beta_row[h : h + 1, :])
-    pseudo = mm_split(scaled, values)
     wy = mm_split(
         per_head(lambda h: scaled[h] * (exp_row[h : h + 1, :] * r_row[h // group])),
         per_head(lambda h: keys[h // group]),
     )
-    wy_pseudo = jnp.concatenate([wy, pseudo], axis=2)
     tails = per_head(
         lambda h: keys_t32[h // group] * (r_row[h // group] * tail_row[h : h + 1, :])
     )
-    moved = mm(tails, wy_pseudo)
+    moved = mm3(tails, wy)
     for h in range(heads):
-        own_t[h] = exp_total[h : h + 1, :] * eye - moved[h, :, :D]
-        own_s[h] = moved[h, :, D:]
-
-    pl.semaphore_wait(barrier, greeted)
-
-    def head_copy(k, own, zin, send, recv):
-        h = (z // 2 + k) % heads
+        own_t[h] = exp_total[h : h + 1, :] * eye - moved[h]
+
+    def head_copy(h, own, zin, send, recv):
         return pltpu.make_async_remote_copy(
             src_ref=own.at[h],
             dst_ref=zin.at[z],
-            send_sem=send.at[k],
+            send_sem=send.at[h],
             recv_sem=recv.at[z],
             device_id=(y * nz + 2 * h + core, head),
             device_id_type=MESH,
         )
 
-    moves = ((own_t, zin_t, zsend_t, zrecv_t), (own_s, zin_s, zsend_s, zrecv_s))
-    by_distance = sorted(range(heads), key=lambda k: -min(k, heads - k))
-    for move in moves:
-        for k in by_distance:
-            if k:
-                head_copy(k, *move).start()
-            else:
-
-                @pl.when(jnp.logical_not(worker))
-                def _():
-                    head_copy(0, *move).start()
-
-                @pl.when(worker)
-                def _():
-                    move[1][pl.ds(z, 1)] = move[0][pl.ds(z // 2, 1)]
-
+    move_t = (own_t, zin_t, zsend_t, zrecv_t)
+    move_s = (own_s, zin_s, zsend_s, zrecv_s)
+
+    def send_head(h, move):
+        @pl.when(z != 2 * h + core)
+        def _():
+            head_copy(h, *move).start()
+
+        @pl.when(z == 2 * h + core)
+        def _():
+            move[1][pl.ds(z, 1)] = move[0][h : h + 1]
+
+    def await_ready(h):
+        for other in (2 * h, 2 * h + 1):
+
+            @pl.when(other > z)
+            def _():
+                pl.semaphore_wait(ready.at[other], 1)
+
+    early = heads // 2
+    for h in range(early):
+        await_ready(h)
+        send_head(h, move_t)
+    loads[3].wait()
+    values = jnp.stack([v_ref[:, i * D : (i + 1) * D] for i in range(heads)])
+    pseudo = mm_split(scaled, values)
+    gained = mm3(tails, pseudo)
+    for h in range(heads):
+        own_s[h] = gained[h]
+    for h in range(early):
+        send_head(h, move_s)
+    for h in range(early, heads):
+        await_ready(h)
+        send_head(h, move_t)
+        send_head(h, move_s)
+
+    loads[4].wait()
+    queries = jnp.stack([q_ref[:, i * D : (i + 1) * D] for i in range(kheads)])
+    scores = mm_bf16(queries, keys_t) * r_row
+    exp_col = jnp.exp(cum_col)
+    wy_pseudo = jnp.concatenate([wy, pseudo], axis=2)
     mixed = mm3(per_head(lambda h: scores[h // group] * decay_mat[h]), wy_pseudo)
     for h in range(heads):
         within[h] = mixed[h, :, D:]
         qmap[h] = exp_col[:, h : h + 1] * queries[h // group].astype(F32) - mixed[h, :, :D]
     for copy in loads[5:]:
         copy.wait()
+    for h in range(heads):
+        gate = gate_ref[:, h * D : (h + 1) * D].astype(F32)
+        gating[h] = gain_ref[...] * (gate / (1.0 + jnp.exp(-gate)))
 
     def row_copy(dy, src, yin, send, recv):
         return pltpu.make_async_remote_copy(
@@ -407,12 +444,10 @@
         def _():
             arrived(sin.at[h], rrecv.at[h])
 
-        core_out = within[h] + mm3(qmap[h], sin[h])
-        normed = core_out * lax.rsqrt(jnp.mean(core_out * core_out, axis=1, keepdims=True) + 1e-06)
-        gate = gate_ref[:, h * D : (h + 1) * D].astype(F32)
-        gated_ref[:, h * D : (h + 1) * D] = (
-            normed * gain_ref[...] * (gate / (1.0 + jnp.exp(-gate)))
-        ).astype(BF16)
+    core_out = within[...] + mm3(qmap[...], sin[...])
+    scale = lax.rsqrt(jnp.mean(core_out * core_out, axis=2, keepdims=True) + 1e-06)
+    for h in range(heads):
+        gated_ref[:, h * D : (h + 1) * D] = (core_out[h] * scale[h] * gating[h]).astype(BF16)
 
     gated = gated_ref[...]
 
@@ -451,21 +486,12 @@
         mine[step] = mine[step] + pair_in[step]
         if step:
             chip_copy(step).start()
-    summed = mine[0]
-    for step in order[1:-1] + order[:-1][:1]:
-        chip_copy(step).wait_recv()
-        summed = summed + chip_in[step]
-    out_ref[...] = summed.astype(BF16)
-
-    for move in moves:
-        for k in range(heads):
-            if k:
-                head_copy(k, *move).wait_send()
-            else:
-
-                @pl.when(jnp.logical_not(worker))
-                def _():
-                    head_copy(0, *move).wait_send()
+    for move in (move_t, move_s):
+        for h in range(heads):
+
+            @pl.when(z != 2 * h + core)
+            def _():
+                head_copy(h, *move).wait_send()
 
     @pl.when(worker)
     def _():
@@ -477,6 +503,14 @@
 
     for step in order:
         pair_copy(step).wait_send()
+
+    summed = mine[0]
+    for step in order[1:-1] + order[:-1][:1]:
+        chip_copy(step).wait_recv()
+        summed = summed + chip_in[step]
+    out_ref[...] = summed.astype(BF16)
+
+    for step in order:
         if step:
             chip_copy(step).wait_send()
 
@@ -525,11 +559,13 @@
             vmem((heads, D, D), F32),
             vmem((heads, D, D), F32),
             vmem((heads, D, D), F32),
+            vmem((heads, D, D), F32),
             vmem((tokens, heads * D), BF16),
             vmem((n // 2, tokens, width), F32),
             vmem((n // 2, tokens, width), F32),
             vmem((n // 2, tokens, width), F32),
             vmem((n // 2, tokens, width), F32),
+            pltpu.SemaphoreType.REGULAR((nz,)),
             dma((len(args),)),
             dma((heads,)),
             dma((heads,)),

time: 58.8 us -> 62.5 us (1.063)
  the two profiles are of different devices: /device:TPU:41 before, /device:TPU:57 now
where the time goes in v4:
time: 62.5 us; the launch traced here: 62.4 us
  Pallas kernels  60.9 us (97%)
  local copies, waits for them, and re-layouts  1.47 us (2%)
    pallas_call x1, Pallas kernels, per_device(): pl.pallas_call(functools.partial(kernel, ny, nz, n), out_shape=jax.ShapeD...  60.9 us
    unnamed x1, local copies, waits for them, and re-layouts  1.47 us

profile of v4, /device:TPU:57, one launch (start us, length us, event | category | flops | bytes accessed | tf_op | source)
XLA Modules:
  0.0 62.4 jit_solution(15491911328761413056)
XLA Ops:
  0.0 60.9 %delta_layer.1 = bf16[128,256]{1,0:T(8,128)(2,1)} custom-call(bf16[128,256]{1,0:T(8,128)(2,1)} %q_hbm.1, bf16[128,256]{1,0:T(8,128)(2,1)} %k_hbm.1, bf16[128,512]{1,0:T(8,128)(2,1)} %v_hbm.1, f32[4,128]{1,0:T(4,128)} %bitcast.3, f32[4,128]{1,0:T(4,128)} %bitcast.4, bf16[128,512]{1,0:T(8,128)(2,1)} %gate_hbm.1, f32[1,128]{1,0:T(1,128)} %bitcast.5, ...), custom_call_target="tpu_custom_call" | custom-call | tf_op jit(solution)/shard_map/delta_layer/pallas_call | solution.py:539
  60.9 1.5 %copy.10 = bf16[128,256]{1,0:T(8,128)(2,1)} copy(bf16[128,256]{1,0:T(8,128)(2,1)} %delta_layer.1) | data formatting | bytes 131072

commit v5 on v4

--- a/solution.py
+++ b/solution.py
@@ -116,7 +116,6 @@
     pair_in,
     mine,
     chip_in,
-    ready,
     load,
     zsend_t,
     zsend_s,
@@ -167,21 +166,14 @@
     def greet(where):
         pl.semaphore_signal(barrier, inc=1, device_id=where, device_id_type=MESH)
 
-    for other in range(1, nz):
-
-        @pl.when(other > z)
-        def _():
-            greet((y * nz + other, head))
-
-    for other in range(ny - 1):
-
-        @pl.when(other < y)
-        def _():
-            greet((other * nz + z, head))
-
+    for dz in range(1, nz):
+        greet((y * nz + (z + dz) % nz, head))
+    for dy in range(1, ny):
+        greet((((y + dy) % ny) * nz + z, head))
     greet((ctx, sibling))
     for dx in range(1, chips):
         greet((ctx, ((x + dx) % chips) * 2 + core))
+    greeted = nz - 1 + ny - 1 + chips
 
     for copy in loads[:3]:
         copy.wait()
@@ -221,15 +213,6 @@
             strict, beta_col[:, h : h + 1] * gram[h // group] * decay_mat[h], 0.0
         )
     )
-    pl.semaphore_wait(barrier, z + (ny - 1 - y) + chips)
-    for other in range(nz - 1):
-
-        @pl.when(other < z)
-        def _():
-            pl.semaphore_signal(
-                ready.at[z], inc=1, device_id=(y * nz + other, head), device_id_type=MESH
-            )
-
     inverse = unit_lower_inverse(strict_part)
     scaled = per_head(lambda h: inverse[h] * beta_row[h : h + 1, :])
     wy = mm_split(
@@ -243,51 +226,45 @@
     for h in range(heads):
         own_t[h] = exp_total[h : h + 1, :] * eye - moved[h]
 
-    def head_copy(h, own, zin, send, recv):
+    pl.semaphore_wait(barrier, greeted)
+
+    def head_copy(k, own, zin, send, recv):
+        h = (z // 2 + k) % heads
         return pltpu.make_async_remote_copy(
             src_ref=own.at[h],
             dst_ref=zin.at[z],
-            send_sem=send.at[h],
+            send_sem=send.at[k],
             recv_sem=recv.at[z],
             device_id=(y * nz + 2 * h + core, head),
             device_id_type=MESH,
         )
 
+    by_distance = sorted(range(heads), key=lambda k: -min(k, heads - k))
     move_t = (own_t, zin_t, zsend_t, zrecv_t)
     move_s = (own_s, zin_s, zsend_s, zrecv_s)
 
-    def send_head(h, move):
-        @pl.when(z != 2 * h + core)
-        def _():
-            head_copy(h, *move).start()
-
-        @pl.when(z == 2 * h + core)
-        def _():
-            move[1][pl.ds(z, 1)] = move[0][h : h + 1]
-
-    def await_ready(h):
-        for other in (2 * h, 2 * h + 1):
-
-            @pl.when(other > z)
-            def _():
-                pl.semaphore_wait(ready.at[other], 1)
-
-    early = heads // 2
-    for h in range(early):
-        await_ready(h)
-        send_head(h, move_t)
+    def send_heads(move):
+        for k in by_distance:
+            if k:
+                head_copy(k, *move).start()
+            else:
+
+                @pl.when(jnp.logical_not(worker))
+                def _():
+                    head_copy(0, *move).start()
+
+                @pl.when(worker)
+                def _():
+                    move[1][pl.ds(z, 1)] = move[0][pl.ds(z // 2, 1)]
+
+    send_heads(move_t)
     loads[3].wait()
     values = jnp.stack([v_ref[:, i * D : (i + 1) * D] for i in range(heads)])
     pseudo = mm_split(scaled, values)
     gained = mm3(tails, pseudo)
     for h in range(heads):
         own_s[h] = gained[h]
-    for h in range(early):
-        send_head(h, move_s)
-    for h in range(early, heads):
-        await_ready(h)
-        send_head(h, move_t)
-        send_head(h, move_s)
+    send_heads(move_s)
 
     loads[4].wait()
     queries = jnp.stack([q_ref[:, i * D : (i + 1) * D] for i in range(kheads)])
@@ -487,11 +464,14 @@
         if step:
             chip_copy(step).start()
     for move in (move_t, move_s):
-        for h in range(heads):
-
-            @pl.when(z != 2 * h + core)
-            def _():
-                head_copy(h, *move).wait_send()
+        for k in range(heads):
+            if k:
+                head_copy(k, *move).wait_send()
+            else:
+
+                @pl.when(jnp.logical_not(worker))
+                def _():
+                    head_copy(0, *move).wait_send()
 
     @pl.when(worker)
     def _():
@@ -565,7 +545,6 @@
             vmem((n // 2, tokens, width), F32),
             vmem((n // 2, tokens, width), F32),
             vmem((n // 2, tokens, width), F32),
-            pltpu.SemaphoreType.REGULAR((nz,)),
             dma((len(args),)),
             dma((heads,)),
             dma((heads,)),

time: 62.5 us -> 57.3 us (0.917)
  Pallas kernels: 60.9 us -> 55.1 us
    pallas_call x1, Pallas kernels: 60.9 us -> 55.1 us  [per_device(): pl.pallas_call(functools.partial(kernel, ny, nz, n), out_shape=jax.ShapeD...]
where the time goes in v5:
time: 57.3 us; the launch traced here: 56.5 us
  Pallas kernels  55.1 us (96%)
  local copies, waits for them, and re-layouts  1.47 us (3%)
    pallas_call x1, Pallas kernels, per_device(): pl.pallas_call(functools.partial(kernel, ny, nz, n), out_shape=jax.ShapeD...  55.1 us
    unnamed x1, local copies, waits for them, and re-layouts  1.47 us

profile of v5, /device:TPU:57, one launch (start us, length us, event | category | flops | bytes accessed | tf_op | source)
XLA Modules:
  0.0 56.5 jit_solution(13196448565380223843)
XLA Ops:
  0.0 55.1 %delta_layer.1 = bf16[128,256]{1,0:T(8,128)(2,1)} custom-call(bf16[128,256]{1,0:T(8,128)(2,1)} %q_hbm.1, bf16[128,256]{1,0:T(8,128)(2,1)} %k_hbm.1, bf16[128,512]{1,0:T(8,128)(2,1)} %v_hbm.1, f32[4,128]{1,0:T(4,128)} %bitcast.3, f32[4,128]{1,0:T(4,128)} %bitcast.4, bf16[128,512]{1,0:T(8,128)(2,1)} %gate_hbm.1, f32[1,128]{1,0:T(1,128)} %bitcast.5, ...), custom_call_target="tpu_custom_call" | custom-call | tf_op jit(solution)/shard_map/delta_layer/pallas_call | solution.py:519
  55.1 1.5 %copy.10 = bf16[128,256]{1,0:T(8,128)(2,1)} copy(bf16[128,256]{1,0:T(8,128)(2,1)} %delta_layer.1) | data formatting | bytes 131072

commit v6 on v5

--- a/solution.py
+++ b/solution.py
@@ -11,6 +11,8 @@
 F32 = jnp.float32
 BF16 = jnp.bfloat16
 D = 128
+PARTS = 2
+ROWS = D // PARTS
 
 
 def mm(a, b):
@@ -40,6 +42,18 @@
     a_high, a_low = cut(a)
     b_high, b_low = cut(b)
     return mm_bf16(a_high, b_high) + (mm_bf16(a_high, b_low) + mm_bf16(a_low, b_high))
+
+
+def nt3(a, b_cut):
+    batch = tuple(range(a.ndim - 2))
+    dims = (((a.ndim - 1,), (a.ndim - 1,)), (batch, batch))
+
+    def dot(left, right):
+        return lax.dot_general(left, right, dims, preferred_element_type=F32)
+
+    a_high, a_low = cut(a)
+    b_high, b_low = b_cut
+    return dot(a_high, b_high) + (dot(a_high, b_low) + dot(a_low, b_high))
 
 
 def nt(a, b):
@@ -102,7 +116,8 @@
     yin_s,
     total_t,
     total_s,
-    prefix_t,
+    prefix_high,
+    prefix_low,
     prefix_s,
     suffix,
     reach,
@@ -228,43 +243,68 @@
 
     pl.semaphore_wait(barrier, greeted)
 
-    def head_copy(k, own, zin, send, recv):
+    def head_copy(k):
         h = (z // 2 + k) % heads
         return pltpu.make_async_remote_copy(
-            src_ref=own.at[h],
-            dst_ref=zin.at[z],
-            send_sem=send.at[k],
-            recv_sem=recv.at[z],
+            src_ref=own_t.at[h],
+            dst_ref=zin_t.at[z],
+            send_sem=zsend_t.at[k],
+            recv_sem=zrecv_t.at[z],
             device_id=(y * nz + 2 * h + core, head),
             device_id_type=MESH,
         )
 
-    by_distance = sorted(range(heads), key=lambda k: -min(k, heads - k))
-    move_t = (own_t, zin_t, zsend_t, zrecv_t)
-    move_s = (own_s, zin_s, zsend_s, zrecv_s)
-
-    def send_heads(move):
+    def part(p):
+        return pl.ds(p * ROWS, ROWS)
+
+    def head_part_copy(k, p):
+        h = (z // 2 + k) % heads
+        return pltpu.make_async_remote_copy(
+            src_ref=own_s.at[h, part(p)],
+            dst_ref=zin_s.at[z, part(p)],
+            send_sem=zsend_s.at[p, k],
+            recv_sem=zrecv_s.at[p, z],
+            device_id=(y * nz + 2 * h + core, head),
+            device_id_type=MESH,
+        )
+
+    def each_head_copy(act):
         for k in by_distance:
             if k:
-                head_copy(k, *move).start()
+                act(head_copy(k))
             else:
 
                 @pl.when(jnp.logical_not(worker))
                 def _():
-                    head_copy(0, *move).start()
-
-                @pl.when(worker)
-                def _():
-                    move[1][pl.ds(z, 1)] = move[0][pl.ds(z // 2, 1)]
-
-    send_heads(move_t)
+                    act(head_copy(0))
+
+    def each_head_part_copy(act):
+        for p in range(PARTS):
+            for k in by_distance:
+                if k:
+                    act(head_part_copy(k, p))
+                else:
+
+                    @pl.when(jnp.logical_not(worker))
+                    def _():
+                        act(head_part_copy(0, p))
+
+    def keep_own(own, zin):
+        @pl.when(worker)
+        def _():
+            zin[pl.ds(z, 1)] = own[pl.ds(z // 2, 1)]
+
+    by_distance = sorted(range(heads), key=lambda k: -min(k, heads - k))
+    each_head_copy(lambda copy: copy.start())
+    keep_own(own_t, zin_t)
     loads[3].wait()
     values = jnp.stack([v_ref[:, i * D : (i + 1) * D] for i in range(heads)])
     pseudo = mm_split(scaled, values)
     gained = mm3(tails, pseudo)
     for h in range(heads):
-        own_s[h] = gained[h]
-    send_heads(move_s)
+        own_s[h] = gained[h].T
+    each_head_part_copy(lambda copy: copy.start())
+    keep_own(own_s, zin_s)
 
     loads[4].wait()
     queries = jnp.stack([q_ref[:, i * D : (i + 1) * D] for i in range(kheads)])
@@ -281,12 +321,22 @@
         gate = gate_ref[:, h * D : (h + 1) * D].astype(F32)
         gating[h] = gain_ref[...] * (gate / (1.0 + jnp.exp(-gate)))
 
-    def row_copy(dy, src, yin, send, recv):
+    def row_copy(dy):
         return pltpu.make_async_remote_copy(
-            src_ref=src,
-            dst_ref=yin.at[dy],
-            send_sem=send.at[dy],
-            recv_sem=recv.at[dy],
+            src_ref=total_t,
+            dst_ref=yin_t.at[dy],
+            send_sem=ysend_t.at[dy],
+            recv_sem=yrecv_t.at[dy],
+            device_id=((y + dy) * nz + z, head),
+            device_id_type=MESH,
+        )
+
+    def row_part_copy(dy, p):
+        return pltpu.make_async_remote_copy(
+            src_ref=total_s.at[part(p)],
+            dst_ref=yin_s.at[dy, part(p)],
+            send_sem=ysend_s.at[p, dy],
+            recv_sem=yrecv_s.at[p, dy],
             device_id=((y + dy) * nz + z, head),
             device_id_type=MESH,
         )
@@ -298,22 +348,22 @@
 
             @pl.when((y > 0) & (y + dy < ny))
             def _():
-                act(row_copy(dy, total_t, yin_t, ysend_t, yrecv_t))
-
-    def each_row_s(act):
+                act(row_copy(dy))
+
+    def each_row_s(act, p):
         for dy in far_rows:
 
             @pl.when(y + dy < ny)
             def _():
-                act(row_copy(dy, total_s, yin_s, ysend_s, yrecv_s))
-
-    def state_copy(dz):
+                act(row_part_copy(dy, p))
+
+    def state_copy(dz, p):
         i = (z + dz) % nz
         return pltpu.make_async_remote_copy(
-            src_ref=sout.at[i],
-            dst_ref=sin.at[z // 2],
-            send_sem=rsend.at[dz],
-            recv_sem=rrecv.at[z // 2],
+            src_ref=sout.at[i, part(p)],
+            dst_ref=sin.at[z // 2, part(p)],
+            send_sem=rsend.at[p, dz],
+            recv_sem=rrecv.at[p, z // 2],
             device_id=(y * nz + i, head),
             device_id_type=MESH,
         )
@@ -332,14 +382,12 @@
 
     @pl.when(worker)
     def _():
-        def wait_place(zin, recv):
-            for i in range(nz):
-
-                @pl.when(z != i)
-                def _():
-                    arrived(zin.at[i], recv.at[i])
-
-        wait_place(zin_t, zrecv_t)
+        for i in range(nz):
+
+            @pl.when(z != i)
+            def _():
+                arrived(zin_t.at[i], zrecv_t.at[i])
+
         first = {(i, i + 1): zin_t[i] for i in range(nz)}
 
         def trans(low, high):
@@ -353,15 +401,22 @@
         each_row_t(lambda copy: copy.start())
         for i in range(1, nz):
             suffix[:, (i - 1) * D : i * D] = trans(i, nz)
-        prefix_t[0] = eye
+        prefix_high[0] = eye.astype(BF16)
+        prefix_low[0] = jnp.zeros((D, D), BF16)
         for i in range(1, nz):
-            prefix_t[i] = trans(0, i)
-
-        wait_place(zin_s, zrecv_s)
-        total_s[...] = zin_s[nz - 1] + mm3(
-            suffix[...], zin_s[: nz - 1].reshape((nz - 1) * D, D)
-        )
-        each_row_s(lambda copy: copy.start())
+            prefix_high[i], prefix_low[i] = cut(trans(0, i))
+
+        suffix_cut = cut(suffix[...])
+        for p in range(PARTS):
+            for i in range(nz):
+
+                @pl.when(z != i)
+                def _():
+                    arrived(zin_s.at[i, part(p)], zrecv_s.at[p, i])
+
+            before = jnp.concatenate([zin_s[i, part(p)] for i in range(nz - 1)], axis=1)
+            total_s[part(p)] = zin_s[nz - 1, part(p)] + nt3(before, suffix_cut)
+            each_row_s(lambda copy: copy.start(), p)
 
         prefix_s[0] = jnp.zeros((D, D), F32)
         states = {(i, i + 1): zin_s[i] for i in range(nz)}
@@ -370,58 +425,70 @@
             if (low, high) not in states:
                 span = 1 << ((high - low - 1).bit_length() - 1)
                 middle = low + span if low % (2 * span) == 0 else high - span
-                states[(low, high)] = mm3(trans(middle, high), state_of(low, middle)) + state_of(
-                    middle, high
-                )
+                states[(low, high)] = nt3(
+                    state_of(low, middle), cut(trans(middle, high))
+                ) + state_of(middle, high)
             return states[(low, high)]
 
         for i in range(1, nz):
             prefix_s[i] = state_of(0, i)
 
-        reach[:, :D] = eye
-        for dy in range(2, ny):
-            here = slice((dy - 1) * D, dy * D)
-            before = slice((dy - 2) * D, (dy - 1) * D)
-
-            @pl.when(dy <= y)
-            def _():
-                arrived(yin_t.at[dy - 1], yrecv_t.at[dy - 1])
-                if dy == 2:
-                    reach[:, here] = yin_t[1]
-                else:
-                    reach[:, here] = mm3(reach[:, before], yin_t[dy - 1])
-
-            @pl.when(dy > y)
-            def _():
-                reach[:, here] = jnp.zeros((D, D), F32)
-
         for dy in range(1, ny):
-
-            @pl.when(dy <= y)
-            def _():
-                arrived(yin_s.at[dy], yrecv_s.at[dy])
 
             @pl.when(dy > y)
             def _():
                 yin_s[dy] = jnp.zeros((D, D), F32)
 
-        state = mm3(reach[...], yin_s[1:].reshape((ny - 1) * D, D))
-        for dz in targets:
-            i = (z + dz) % nz
-            result = mm3(prefix_t[pl.ds(i, 1)][0], state) + prefix_s[pl.ds(i, 1)][0]
-            if dz:
-                sout[pl.ds(i, 1)] = result[None]
-                state_copy(dz).start()
-            else:
-                sin[pl.ds(z // 2, 1)] = result[None]
+            @pl.when(dy >= y)
+            def _():
+                yin_t[dy] = eye
+
+            @pl.when(dy < y)
+            def _():
+                arrived(yin_t.at[dy], yrecv_t.at[dy])
+
+        paths = {(dy, dy + 1): yin_t[dy] for dy in range(1, ny - 1)}
+
+        def path(low, high):
+            if (low, high) not in paths:
+                span = 1 << ((high - low - 1).bit_length() - 1)
+                paths[(low, high)] = mm3(path(low, low + span), path(low + span, high))
+            return paths[(low, high)]
+
+        reach[:, :D] = eye
+        for dy in range(2, ny):
+            reach[:, (dy - 1) * D : dy * D] = path(1, dy)
+        reach_cut = cut(reach[...])
+        for p in range(PARTS):
+            for dy in range(1, ny):
+
+                @pl.when(dy <= y)
+                def _():
+                    arrived(yin_s.at[dy, part(p)], yrecv_s.at[p, dy])
+
+            rows_in = jnp.concatenate([yin_s[dy, part(p)] for dy in range(1, ny)], axis=1)
+            state = nt3(rows_in, reach_cut)
+            for dz in targets:
+                i = (z + dz) % nz
+                one = pl.ds(i, 1)
+                result = (
+                    nt3(state, (prefix_high[one][0], prefix_low[one][0]))
+                    + prefix_s[one, part(p)][0]
+                )
+                if dz:
+                    sout[one, part(p)] = result[None]
+                    state_copy(dz, p).start()
+                else:
+                    sin[pl.ds(z // 2, 1), part(p)] = result[None]
 
     for h in range(heads):
 
         @pl.when(jnp.logical_not(worker) | (z // 2 != h))
         def _():
-            arrived(sin.at[h], rrecv.at[h])
-
-    core_out = within[...] + mm3(qmap[...], sin[...])
+            for p in range(PARTS):
+                arrived(sin.at[h, part(p)], rrecv.at[p, h])
+
+    core_out = within[...] + nt3(qmap[...], cut(sin[...]))
     scale = lax.rsqrt(jnp.mean(core_out * core_out, axis=2, keepdims=True) + 1e-06)
     for h in range(heads):
         gated_ref[:, h * D : (h + 1) * D] = (core_out[h] * scale[h] * gating[h]).astype(BF16)
@@ -463,23 +530,17 @@
         mine[step] = mine[step] + pair_in[step]
         if step:
             chip_copy(step).start()
-    for move in (move_t, move_s):
-        for k in range(heads):
-            if k:
-                head_copy(k, *move).wait_send()
-            else:
-
-                @pl.when(jnp.logical_not(worker))
-                def _():
-                    head_copy(0, *move).wait_send()
+    each_head_copy(lambda copy: copy.wait_send())
+    each_head_part_copy(lambda copy: copy.wait_send())
 
     @pl.when(worker)
     def _():
         each_row_t(lambda copy: copy.wait_send())
-        each_row_s(lambda copy: copy.wait_send())
-        for dz in targets:
-            if dz:
-                state_copy(dz).wait_send()
+        for p in range(PARTS):
+            each_row_s(lambda copy: copy.wait_send(), p)
+            for dz in targets:
+                if dz:
+                    state_copy(dz, p).wait_send()
 
     for step in order:
         pair_copy(step).wait_send()
@@ -531,7 +592,8 @@
             vmem((ny, D, D), F32),
             vmem((D, D), F32),
             vmem((D, D), F32),
-            vmem((nz, D, D), F32),
+            vmem((nz, D, D), BF16),
+            vmem((nz, D, D), BF16),
             vmem((nz, D, D), F32),
             vmem((D, (nz - 1) * D), F32),
             vmem((D, (ny - 1) * D), F32),
@@ -547,15 +609,15 @@
             vmem((n // 2, tokens, width), F32),
             dma((len(args),)),
             dma((heads,)),
-            dma((heads,)),
+            dma((PARTS, heads)),
             dma((nz,)),
-            dma((nz,)),
+            dma((PARTS, nz)),
             dma((ny,)),
+            dma((PARTS, ny)),
             dma((ny,)),
-            dma((ny,)),
-            dma((ny,)),
-            dma((nz,)),
-            dma((heads,)),
+            dma((PARTS, ny)),
+            dma((PARTS, nz)),
+            dma((PARTS, heads)),
             dma((n // 2,)),
             dma((n // 2,)),
             dma((n // 2,)),

time: 57.3 us -> 56.2 us (0.981)
  Pallas kernels: 55.1 us -> 54.2 us
    pallas_call x1, Pallas kernels: 55.1 us -> 54.2 us  [per_device(): pl.pallas_call(functools.partial(kernel, ny, nz, n), out_shape=jax.ShapeD...]
where the time goes in v6:
time: 56.2 us; the launch traced here: 55.7 us
  Pallas kernels  54.2 us (96%)
  local copies, waits for them, and re-layouts  1.47 us (3%)
    pallas_call x1, Pallas kernels, per_device(): pl.pallas_call(functools.partial(kernel, ny, nz, n), out_shape=jax.ShapeD...  54.2 us
    unnamed x1, local copies, waits for them, and re-layouts  1.47 us

profile of v6, /device:TPU:57, one launch (start us, length us, event | category | flops | bytes accessed | tf_op | source)
XLA Modules:
  0.0 55.7 jit_solution(375884044578970037)
XLA Ops:
  0.0 54.2 %delta_layer.1 = bf16[128,256]{1,0:T(8,128)(2,1)} custom-call(bf16[128,256]{1,0:T(8,128)(2,1)} %q_hbm.1, bf16[128,256]{1,0:T(8,128)(2,1)} %k_hbm.1, bf16[128,512]{1,0:T(8,128)(2,1)} %v_hbm.1, f32[4,128]{1,0:T(4,128)} %bitcast.3, f32[4,128]{1,0:T(4,128)} %bitcast.4, bf16[128,512]{1,0:T(8,128)(2,1)} %gate_hbm.1, f32[1,128]{1,0:T(1,128)} %bitcast.5, ...), custom_call_target="tpu_custom_call" | custom-call | tf_op jit(solution)/shard_map/delta_layer/pallas_call | solution.py:580
  54.2 1.5 %copy.10 = bf16[128,256]{1,0:T(8,128)(2,1)} copy(bf16[128,256]{1,0:T(8,128)(2,1)} %delta_layer.1) | data formatting | bytes 131072

commit v7 on v6

--- a/solution.py
+++ b/solution.py
@@ -131,6 +131,7 @@
     pair_in,
     mine,
     chip_in,
+    ready,
     load,
     zsend_t,
     zsend_s,
@@ -181,14 +182,21 @@
     def greet(where):
         pl.semaphore_signal(barrier, inc=1, device_id=where, device_id_type=MESH)
 
-    for dz in range(1, nz):
-        greet((y * nz + (z + dz) % nz, head))
-    for dy in range(1, ny):
-        greet((((y + dy) % ny) * nz + z, head))
+    for other in range(1, nz):
+
+        @pl.when(other > z)
+        def _():
+            greet((y * nz + other, head))
+
+    for other in range(ny - 1):
+
+        @pl.when(other < y)
+        def _():
+            greet((other * nz + z, head))
+
     greet((ctx, sibling))
     for dx in range(1, chips):
         greet((ctx, ((x + dx) % chips) * 2 + core))
-    greeted = nz - 1 + ny - 1 + chips
 
     for copy in loads[:3]:
         copy.wait()
@@ -228,6 +236,15 @@
             strict, beta_col[:, h : h + 1] * gram[h // group] * decay_mat[h], 0.0
         )
     )
+    pl.semaphore_wait(barrier, z + (ny - 1 - y) + chips)
+    for other in range(nz - 1):
+
+        @pl.when(other < z)
+        def _():
+            pl.semaphore_signal(
+                ready.at[z], inc=1, device_id=(y * nz + other, head), device_id_type=MESH
+            )
+
     inverse = unit_lower_inverse(strict_part)
     scaled = per_head(lambda h: inverse[h] * beta_row[h : h + 1, :])
     wy = mm_split(
@@ -241,14 +258,11 @@
     for h in range(heads):
         own_t[h] = exp_total[h : h + 1, :] * eye - moved[h]
 
-    pl.semaphore_wait(barrier, greeted)
-
-    def head_copy(k):
-        h = (z // 2 + k) % heads
+    def head_copy(h):
         return pltpu.make_async_remote_copy(
             src_ref=own_t.at[h],
             dst_ref=zin_t.at[z],
-            send_sem=zsend_t.at[k],
+            send_sem=zsend_t.at[h],
             recv_sem=zrecv_t.at[z],
             device_id=(y * nz + 2 * h + core, head),
             device_id_type=MESH,
@@ -268,15 +282,15 @@
             device_id_type=MESH,
         )
 
-    def each_head_copy(act):
-        for k in by_distance:
-            if k:
-                act(head_copy(k))
-            else:
-
-                @pl.when(jnp.logical_not(worker))
-                def _():
-                    act(head_copy(0))
+    by_distance = sorted(range(heads), key=lambda k: -min(k, heads - k))
+
+    def each_head_copy(act, before=lambda h: None):
+        for h in range(heads):
+            before(h)
+
+            @pl.when(z != 2 * h + core)
+            def _():
+                act(head_copy(h))
 
     def each_head_part_copy(act):
         for p in range(PARTS):
@@ -289,13 +303,19 @@
                     def _():
                         act(head_part_copy(0, p))
 
+    def await_ready(h):
+        for other in (2 * h, 2 * h + 1):
+
+            @pl.when(other > z)
+            def _():
+                pl.semaphore_wait(ready.at[other], 1)
+
     def keep_own(own, zin):
         @pl.when(worker)
         def _():
             zin[pl.ds(z, 1)] = own[pl.ds(z // 2, 1)]
 
-    by_distance = sorted(range(heads), key=lambda k: -min(k, heads - k))
-    each_head_copy(lambda copy: copy.start())
+    each_head_copy(lambda copy: copy.start(), await_ready)
     keep_own(own_t, zin_t)
     loads[3].wait()
     values = jnp.stack([v_ref[:, i * D : (i + 1) * D] for i in range(heads)])
@@ -579,7 +599,7 @@
     )
     return pl.pallas_call(
         functools.partial(kernel, ny, nz, n),
-        out_shape=jax.ShapeDtypeStruct((tokens, width), BF16),
+        out_shape=vmem((tokens, width), BF16),
         in_specs=[pl.BlockSpec(memory_space=pltpu.HBM)] * len(args),
         out_specs=pl.BlockSpec(memory_space=vmem),
         scratch_shapes=[vmem(a.shape, a.dtype) for a in args]
@@ -607,6 +627,7 @@
             vmem((n // 2, tokens, width), F32),
             vmem((n // 2, tokens, width), F32),
             vmem((n // 2, tokens, width), F32),
+            pltpu.SemaphoreType.REGULAR((nz,)),
             dma((len(args),)),
             dma((heads,)),
             dma((PARTS, heads)),

time: 56.2 us -> 59 us (1.050)
  Pallas kernels: 54.2 us -> 58.3 us
  local copies, waits for them, and re-layouts: 1.47 us -> 0.63 us
    pallas_call x1, Pallas kernels: 54.2 us -> 58.3 us  [per_device(): pl.pallas_call(functools.partial(kernel, ny, nz, n), out_shape=vmem((toke...]
    unnamed x1, local copies, waits for them, and re-layouts: 1.47 us -> 0.63 us
where the time goes in v7:
time: 59 us; the launch traced here: 58.9 us
  Pallas kernels  58.3 us (99%)
  local copies, waits for them, and re-layouts  0.63 us (1%)
    pallas_call x1, Pallas kernels, per_device(): pl.pallas_call(functools.partial(kernel, ny, nz, n), out_shape=vmem((toke...  58.3 us

profile of v7, /device:TPU:57, one launch (start us, length us, event | category | flops | bytes accessed | tf_op | source)
XLA Modules:
  0.0 58.9 jit_solution(9264456716292002422)
XLA Ops:
  0.0 58.3 %delta_layer.1 = bf16[128,256]{1,0:T(8,128)(2,1)S(1)} custom-call(bf16[128,256]{1,0:T(8,128)(2,1)} %q_hbm.1, bf16[128,256]{1,0:T(8,128)(2,1)} %k_hbm.1, bf16[128,512]{1,0:T(8,128)(2,1)} %v_hbm.1, f32[4,128]{1,0:T(4,128)} %bitcast.3, f32[4,128]{1,0:T(4,128)} %bitcast.4, bf16[128,512]{1,0:T(8,128)(2,1)} %gate_hbm.1, f32[1,128]{1,0:T(1,128)} %bitcast.5, ...), custom_call_target="tpu_custom_call" | custom-call | tf_op jit(solution)/shard_map/delta_layer/pallas_call | solution.py:600
  58.3 0.6 %copy.10 = bf16[128,256]{1,0:T(8,128)(2,1)} copy(bf16[128,256]{1,0:T(8,128)(2,1)S(1)} %delta_layer.1) | data formatting | bytes 131072

commit v8 on v6

--- a/solution.py
+++ b/solution.py
@@ -579,7 +579,7 @@
     )
     return pl.pallas_call(
         functools.partial(kernel, ny, nz, n),
-        out_shape=jax.ShapeDtypeStruct((tokens, width), BF16),
+        out_shape=vmem((tokens, width), BF16),
         in_specs=[pl.BlockSpec(memory_space=pltpu.HBM)] * len(args),
         out_specs=pl.BlockSpec(memory_space=vmem),
         scratch_shapes=[vmem(a.shape, a.dtype) for a in args]

time: 56.2 us -> 54.7 us (0.973)
  local copies, waits for them, and re-layouts: 1.47 us -> 0.63 us
  Pallas kernels: 54.2 us -> 53.6 us
    unnamed x1, local copies, waits for them, and re-layouts: 1.47 us -> 0.63 us
    pallas_call x1, Pallas kernels: 54.2 us -> 53.6 us  [per_device(): pl.pallas_call(functools.partial(kernel, ny, nz, n), out_shape=vmem((toke...]
where the time goes in v8:
time: 54.7 us; the launch traced here: 54.3 us
  Pallas kernels  53.6 us (98%)
  local copies, waits for them, and re-layouts  0.63 us (1%)
    pallas_call x1, Pallas kernels, per_device(): pl.pallas_call(functools.partial(kernel, ny, nz, n), out_shape=vmem((toke...  53.6 us

profile of v8, /device:TPU:57, one launch (start us, length us, event | category | flops | bytes accessed | tf_op | source)
XLA Modules:
  0.0 54.3 jit_solution(2498477359708438849)
XLA Ops:
  0.0 53.6 %delta_layer.1 = bf16[128,256]{1,0:T(8,128)(2,1)S(1)} custom-call(bf16[128,256]{1,0:T(8,128)(2,1)} %q_hbm.1, bf16[128,256]{1,0:T(8,128)(2,1)} %k_hbm.1, bf16[128,512]{1,0:T(8,128)(2,1)} %v_hbm.1, f32[4,128]{1,0:T(4,128)} %bitcast.3, f32[4,128]{1,0:T(4,128)} %bitcast.4, bf16[128,512]{1,0:T(8,128)(2,1)} %gate_hbm.1, f32[1,128]{1,0:T(1,128)} %bitcast.5, ...), custom_call_target="tpu_custom_call" | custom-call | tf_op jit(solution)/shard_map/delta_layer/pallas_call | solution.py:580
  53.6 0.6 %copy.10 = bf16[128,256]{1,0:T(8,128)(2,1)} copy(bf16[128,256]{1,0:T(8,128)(2,1)S(1)} %delta_layer.1) | data formatting | bytes 131072

commit v9 on v8

--- a/solution.py
+++ b/solution.py
@@ -173,7 +173,7 @@
             ]
         )
     ]
-    for copy in loads:
+    for copy in loads[:5]:
         copy.start()
 
     barrier = pltpu.get_barrier_semaphore()
@@ -192,6 +192,8 @@
 
     for copy in loads[:3]:
         copy.wait()
+    for copy in loads[5:]:
+        copy.start()
 
     row, col = iotas(D)
     causal, strict = row >= col, row > col
@@ -244,7 +246,7 @@
     pl.semaphore_wait(barrier, greeted)
 
     def head_copy(k):
-        h = (z // 2 + k) % heads
+        h = (z // 2 + k * (1 - 2 * (z % 2)) + heads) % heads
         return pltpu.make_async_remote_copy(
             src_ref=own_t.at[h],
             dst_ref=zin_t.at[z],
@@ -258,7 +260,7 @@
         return pl.ds(p * ROWS, ROWS)
 
     def head_part_copy(k, p):
-        h = (z // 2 + k) % heads
+        h = (z // 2 + k * (1 - 2 * (z % 2)) + heads) % heads
         return pltpu.make_async_remote_copy(
             src_ref=own_s.at[h, part(p)],
             dst_ref=zin_s.at[z, part(p)],
@@ -481,14 +483,17 @@
                 else:
                     sin[pl.ds(z // 2, 1), part(p)] = result[None]
 
-    for h in range(heads):
-
-        @pl.when(jnp.logical_not(worker) | (z // 2 != h))
-        def _():
-            for p in range(PARTS):
+    pieces = []
+    for p in range(PARTS):
+        for h in range(heads):
+
+            @pl.when(jnp.logical_not(worker) | (z // 2 != h))
+            def _():
                 arrived(sin.at[h, part(p)], rrecv.at[p, h])
 
-    core_out = within[...] + nt3(qmap[...], cut(sin[...]))
+        pieces.append(nt3(qmap[...], cut(sin[:, part(p)])))
+
+    core_out = within[...] + jnp.concatenate(pieces, axis=2)
     scale = lax.rsqrt(jnp.mean(core_out * core_out, axis=2, keepdims=True) + 1e-06)
     for h in range(heads):
         gated_ref[:, h * D : (h + 1) * D] = (core_out[h] * scale[h] * gating[h]).astype(BF16)

time: 54.7 us -> 54.7 us (level)
  no operation moved by 1% of the time
where the time goes in v9:
time: 54.7 us; the launch traced here: 54.3 us
  Pallas kernels  53.6 us (98%)
  local copies, waits for them, and re-layouts  0.63 us (1%)
    pallas_call x1, Pallas kernels, per_device(): pl.pallas_call(functools.partial(kernel, ny, nz, n), out_shape=vmem((toke...  53.6 us

profile of v9, /device:TPU:57, one launch (start us, length us, event | category | flops | bytes accessed | tf_op | source)
XLA Modules:
  0.0 54.3 jit_solution(2031927649023940590)
XLA Ops:
  0.0 53.6 %delta_layer.1 = bf16[128,256]{1,0:T(8,128)(2,1)S(1)} custom-call(bf16[128,256]{1,0:T(8,128)(2,1)} %q_hbm.1, bf16[128,256]{1,0:T(8,128)(2,1)} %k_hbm.1, bf16[128,512]{1,0:T(8,128)(2,1)} %v_hbm.1, f32[4,128]{1,0:T(4,128)} %bitcast.3, f32[4,128]{1,0:T(4,128)} %bitcast.4, bf16[128,512]{1,0:T(8,128)(2,1)} %gate_hbm.1, f32[1,128]{1,0:T(1,128)} %bitcast.5, ...), custom_call_target="tpu_custom_call" | custom-call | tf_op jit(solution)/shard_map/delta_layer/pallas_call | solution.py:585
  53.6 0.6 %copy.10 = bf16[128,256]{1,0:T(8,128)(2,1)} copy(bf16[128,256]{1,0:T(8,128)(2,1)S(1)} %delta_layer.1) | data formatting | bytes 131072

commit v10 on v8

--- a/solution.py
+++ b/solution.py
@@ -260,8 +260,8 @@
     def head_part_copy(k, p):
         h = (z // 2 + k) % heads
         return pltpu.make_async_remote_copy(
-            src_ref=own_s.at[h, part(p)],
-            dst_ref=zin_s.at[z, part(p)],
+            src_ref=own_s.at[h],
+            dst_ref=zin_s.at[z],
             send_sem=zsend_s.at[p, k],
             recv_sem=zrecv_s.at[p, z],
             device_id=(y * nz + 2 * h + core, head),
@@ -279,7 +279,7 @@
                     act(head_copy(0))
 
     def each_head_part_copy(act):
-        for p in range(PARTS):
+        for p in range(1):
             for k in by_distance:
                 if k:
                     act(head_part_copy(k, p))
@@ -408,11 +408,11 @@
 
         suffix_cut = cut(suffix[...])
         for p in range(PARTS):
-            for i in range(nz):
+            for i in range(nz if p == 0 else 0):
 
                 @pl.when(z != i)
                 def _():
-                    arrived(zin_s.at[i, part(p)], zrecv_s.at[p, i])
+                    arrived(zin_s.at[i], zrecv_s.at[p, i])
 
             before = jnp.concatenate([zin_s[i, part(p)] for i in range(nz - 1)], axis=1)
             total_s[part(p)] = zin_s[nz - 1, part(p)] + nt3(before, suffix_cut)

time: 54.7 us -> 55.3 us (1.011)
  Pallas kernels: 53.6 us -> 54.3 us
    pallas_call x1, Pallas kernels: 53.6 us -> 54.3 us  [per_device(): pl.pallas_call(functools.partial(kernel, ny, nz, n), out_shape=vmem((toke...]
where the time goes in v10:
time: 55.3 us; the launch traced here: 55 us
  Pallas kernels  54.3 us (98%)
  local copies, waits for them, and re-layouts  0.63 us (1%)
    pallas_call x1, Pallas kernels, per_device(): pl.pallas_call(functools.partial(kernel, ny, nz, n), out_shape=vmem((toke...  54.3 us

profile of v10, /device:TPU:57, one launch (start us, length us, event | category | flops | bytes accessed | tf_op | source)
XLA Modules:
  0.0 55.0 jit_solution(1257244586000467070)
XLA Ops:
  0.0 54.3 %delta_layer.1 = bf16[128,256]{1,0:T(8,128)(2,1)S(1)} custom-call(bf16[128,256]{1,0:T(8,128)(2,1)} %q_hbm.1, bf16[128,256]{1,0:T(8,128)(2,1)} %k_hbm.1, bf16[128,512]{1,0:T(8,128)(2,1)} %v_hbm.1, f32[4,128]{1,0:T(4,128)} %bitcast.3, f32[4,128]{1,0:T(4,128)} %bitcast.4, bf16[128,512]{1,0:T(8,128)(2,1)} %gate_hbm.1, f32[1,128]{1,0:T(1,128)} %bitcast.5, ...), custom_call_target="tpu_custom_call" | custom-call | tf_op jit(solution)/shard_map/delta_layer/pallas_call | solution.py:580
  54.3 0.6 %copy.10 = bf16[128,256]{1,0:T(8,128)(2,1)} copy(bf16[128,256]{1,0:T(8,128)(2,1)S(1)} %delta_layer.1) | data formatting | bytes 131072
